TPU v7x, 256 devices: a whole 4x4x8 slice. The times are simulated.
256 devices in a mesh: ta: 8 (over z), ha: 32 (over x, y, core).
Axes of the slice: x: 4, y: 4, z: 8, core: 2. Of those that a mesh axis runs over, the one named last changes fastest.
Arguments:
- mode_record: bfloat16 [300, 16384], P(None, ('ta', 'ha')), may hold values from -18 to 18
- mode_shapes: bfloat16 [300, 12288], P(None, 'ha'), may hold values from -2.5 to 2.5
- map_elem: int32 [4, 16384], P(None, 'ha'), may hold values from 0 to 383
- map_coef: float32 [4, 16384], P(None, 'ha'), may hold values from -3 to 3
- hot_owner: int32 [8192], P(('ta', 'ha')), may hold values from 0 to 31, as said below
- band_bins: int32 [512], replicated, may hold values from 1 to 64, 8192 in all
Outputs:
- elem_rms: float32 [12288], P('ha')
- band_power: float32 [8192, 512], P(('ta', 'ha'))
Inputs may be any that keep to these rules, and one draw needn't show every extreme that they name: hot_owner[h] is the region whose map slots describe hotspot h. In each aligned block of 32 hotspots (the hotspots of one device) no region owns more than 2, and one region, the same for every block, owns exactly 2 of each block. `map_elem`: slots that no hotspot's map slot names are never read. `band_bins`: the bands follow each other from bin 0 and together cover the 8192 bins below the Nyquist bin.
All inputs are finite; a program needn't handle non-finite values.
Results may differ from a plain program's by a relative error of at most 0.004.
Values may be sent and summed in bfloat16 or wider, within the bound.
A program may use at most 64 MiB of HBM per device.

v0:
```python
import jax
import jax.numpy as jnp
from jax import lax
from jax.sharding import PartitionSpec as P

DFT_LEN = 128
NB = 512
K_EXT = 4
HS_DEV = 32
NT = 16384


epsilon = 1e-06


def first_table(length):
    positions = jnp.arange(length, dtype=jnp.int32)
    angles = (positions[:, None] * positions[None, :] % length).astype(jnp.float32) * (
        2.0 * jnp.pi / length
    )
    return jnp.concatenate([jnp.cos(angles), -jnp.sin(angles)], axis=1).astype(jnp.bfloat16)


def twiddle_table(length, points):
    positions = jnp.arange(length, dtype=jnp.int32)
    angles = (positions[:, None] * positions[None, :]).astype(jnp.float32) * (2.0 * jnp.pi / points)
    return (jnp.cos(angles), jnp.sin(angles))


def second_table(length):
    positions = jnp.arange(length, dtype=jnp.int32)
    halves = jnp.arange(length // 2, dtype=jnp.int32)
    angles = (positions[:, None] * halves[None, :] % length).astype(jnp.float32) * (
        2.0 * jnp.pi / length
    )
    cos_part = jnp.cos(angles).astype(jnp.bfloat16)
    sin_part = jnp.sin(angles).astype(jnp.bfloat16)
    real_row = jnp.stack([cos_part, -sin_part], axis=1)
    imag_row = jnp.stack([sin_part, cos_part], axis=1)
    return jnp.stack([real_row, imag_row], axis=1)


def band_spectrum(series, band_bins):
    row_count = series.shape[0]
    points = DFT_LEN * DFT_LEN
    folded = series.reshape(row_count, DFT_LEN, DFT_LEN)
    section_one = jnp.einsum(
        "hab,ak->hbk", folded, first_table(DFT_LEN), preferred_element_type=jnp.float32
    )
    turn_cos, turn_sin = twiddle_table(DFT_LEN, points)
    real_part = section_one[:, :, :DFT_LEN]
    imag_part = section_one[:, :, DFT_LEN:]
    twiddled = jnp.stack(
        [real_part * turn_cos + imag_part * turn_sin, imag_part * turn_cos - real_part * turn_sin],
        axis=2,
    ).astype(jnp.bfloat16)
    spectrum = jnp.einsum(
        "hbrk,brsq->hqsk", twiddled, second_table(DFT_LEN), preferred_element_type=jnp.float32
    )
    power_bins = (
        spectrum[:, :, 0, :] * spectrum[:, :, 0, :] + spectrum[:, :, 1, :] * spectrum[:, :, 1, :]
    ).astype(jnp.bfloat16)
    bins_half = points // 2
    power_bins = power_bins.reshape(row_count, bins_half)
    span_bins = min(1024, bins_half)
    band_ends = jnp.cumsum(band_bins)
    band_starts = band_ends - band_bins

    def add_block(block_number, running):
        first_bin = block_number * span_bins
        part_power = lax.dynamic_slice_in_dim(power_bins, first_bin, span_bins, 1)
        bin_ids = first_bin + jnp.arange(span_bins, dtype=jnp.int32)
        member = (
            (bin_ids[:, None] >= band_starts[None, :]) & (bin_ids[:, None] < band_ends[None, :])
        ).astype(jnp.bfloat16)
        return running + jnp.dot(part_power, member, preferred_element_type=jnp.float32)

    band_sums = lax.fori_loop(
        0, bins_half // span_bins, add_block, jnp.zeros((row_count, NB), jnp.float32)
    )
    return band_sums / (points * band_bins.astype(jnp.float32))[None, :]


def rank_in_block(owners, regions):
    onehot = (owners[:, None] == jnp.arange(regions, dtype=jnp.int32)[None, :]).astype(jnp.int32)
    before = jnp.cumsum(onehot, axis=0) - onehot
    return jnp.sum(before * onehot, axis=1)


def shards(mode_record, mode_shapes, map_elem, map_coef, hot_owner, band_bins):
    regions = lax.axis_size("ha")
    windows = lax.axis_size("ta")
    per_slot = 2 * HS_DEV // regions
    slot_count = regions * per_slot
    local_rank = rank_in_block(hot_owner, regions)
    pick_rows = hot_owner * per_slot + local_rank
    stress = lax.dot_general(
        mode_shapes,
        lax.all_gather(mode_record, "ha", axis=1, tiled=True),
        (((0,), (0,)), ((), ())),
        preferred_element_type=jnp.float32,
    )
    slot_rows = map_coef[0][:, None] * jnp.take(stress, map_elem[0], axis=0)
    for term_index in range(1, K_EXT):
        slot_rows = slot_rows + map_coef[term_index][:, None] * jnp.take(
            stress, map_elem[term_index], axis=0
        )
    sending = slot_rows.astype(jnp.bfloat16).reshape(windows, regions, per_slot, stress.shape[1])
    arrived = lax.all_to_all(
        lax.all_to_all(sending, "ta", split_axis=0, concat_axis=3, tiled=True),
        "ha",
        split_axis=1,
        concat_axis=1,
        tiled=True,
    )
    arrived = arrived.reshape(slot_count, arrived.shape[3])
    series = jnp.take(arrived, pick_rows, axis=0)
    energy = lax.psum(jnp.sum(stress * stress, axis=1), "ta")
    elem_rms = jnp.sqrt(energy / NT + epsilon)
    band_power = band_spectrum(series, band_bins)
    return (elem_rms, band_power)


def solution(mesh):
    in_specs = (
        P(None, ("ta", "ha")),
        P(None, "ha"),
        P(None, "ha"),
        P(None, "ha"),
        P(("ta", "ha")),
        P(),
    )
    out_specs = (P("ha"), P(("ta", "ha"), None))
    return jax.shard_map(shards, mesh=mesh, in_specs=in_specs, out_specs=out_specs, check_vma=False)
```

profile of v0, /device:TPU:1, one launch (start us, length us, event | category | flops | bytes accessed | tf_op | source)
XLA Modules:
  0.0 209.4 jit_solution(9441090781847248508)
XLA Ops:
  7.2 0.0 copy-start
  7.2 0.0 all-gather.2.cloned.1.call-start
  7.2 0.7 all-gather.2.cloned.1.call-update
  7.9 0.9 fusion.50
  8.9 0.9 fusion.49
  9.8 53.3 %all-gather.2.cloned.1.call-done = bf16[300,2048]{0,1:T(8,128)(2,1)} async-done(((bf16[300,64]{0,1:T(8,128)(2,1)}), bf16[300,2048]{0,1:T(8,128)(2,1)}) %all-gather.2.cloned.1.call-update) | async-done | bytes 1228816 | tf_op jit(solution)/shard_map/all_gather | solution.py:99
  63.1 0.0 copy-done
  63.1 2.5 %multiply_reduce_fusion = (f32[384]{0:T(512)S(1)}, f32[384,2048]{1,0:T(8,128)S(1)}) fusion(bf16[300,384]{1,0:T(8,128)(2,1)S(1)} %copy-done, bf16[300,2048]{0,1:T(8,128)(2,1)} %all-gather.2.cloned.1.call-done), kind=kOutput, calls=%fused_computation.22 | convolution fusion | flops 473431680 | bytes 4606464 | tf_op jit(solution)/shard_map/dot_general | solution.py:97
  65.6 3.6 %gather_fusion.1 = f32[512,2048]{1,0:T(8,128)} fusion(f32[384,2048]{1,0:T(8,128)S(1)} %get-tuple-element.143, s32[1024]{0:T(1024)S(1)} %pad_clamp_fusion.4), kind=kCustom, calls=%fused_computation.clone | custom fusion | bytes 8390656 | tf_op jit(solution)/shard_map/jit(_take)/gather | solution.py:103
  69.2 3.6 %gather_fusion.2 = f32[512,2048]{1,0:T(8,128)} fusion(f32[384,2048]{1,0:T(8,128)S(1)} %get-tuple-element.143, s32[1024]{0:T(1024)S(1)} %pad_clamp_fusion.3), kind=kCustom, calls=%fused_computation.1.clone | custom fusion | bytes 8390656 | tf_op jit(solution)/shard_map/jit(_take)/gather | solution.py:105
  72.8 3.6 %gather_fusion.3 = f32[512,2048]{1,0:T(8,128)} fusion(f32[384,2048]{1,0:T(8,128)S(1)} %get-tuple-element.143, s32[1024]{0:T(1024)S(1)} %pad_clamp_fusion.2), kind=kCustom, calls=%fused_computation.2.clone | custom fusion | bytes 8390656 | tf_op jit(solution)/shard_map/jit(_take)/gather | solution.py:105
  76.4 3.6 %gather_fusion.4 = f32[512,2048]{1,0:T(8,128)} fusion(f32[384,2048]{1,0:T(8,128)S(1)} %get-tuple-element.143, s32[1024]{0:T(1024)S(1)} %pad_clamp_fusion.1), kind=kCustom, calls=%fused_computation.3.clone | custom fusion | bytes 8390656 | tf_op jit(solution)/shard_map/jit(_take)/gather | solution.py:105
  80.0 6.9 %fusion.8 = bf16[512,2048]{1,0:T(8,128)(2,1)S(1)} fusion(f32[512,2048]{1,0:T(8,128)} %gather_fusion.4, f32[512,2048]{1,0:T(8,128)} %gather_fusion.3, f32[512,2048]{1,0:T(8,128)} %gather_fusion.2, f32[512,2048]{1,0:T(8,128)} %gather_fusion.1, f32[512]{0:T(512)S(1)} %bitcast.73, f32[512]{0:T(512)S(1)} %bitcast.74, f32[512]{0:T(512)S(1)} %bitcast.72, ...), kind=kLoop, calls=%fused_computation.16 | loop fusion | flops 12582912 | bytes 18884608 | tf_op jit(solution)/shard_map/convert_element_type | solution.py:108
  86.9 2.6 %reshape.166 = bf16[8,32,2,2048]{3,2,1,0:T(2,128)(2,1)} reshape(bf16[512,2048]{1,0:T(8,128)(2,1)S(1)} %fusion.8) | data formatting | bytes 4194304 | tf_op jit(solution)/shard_map/reshape | solution.py:108
  89.5 2.5 %copy.17 = bf16[8,32,2,2048]{3,1,2,0:T(8,128)(2,1)S(1)} copy(bf16[8,32,2,2048]{3,2,1,0:T(2,128)(2,1)} %reshape.166) | data formatting | bytes 4194304 | tf_op jit(solution)/shard_map/reshape | solution.py:108
  92.0 57.9 %all_to_all.23 = bf16[8,32,2,2048]{3,1,2,0:T(8,128)(2,1)S(1)} all-to-all(bf16[8,32,2,2048]{3,1,2,0:T(8,128)(2,1)S(1)} %copy.17), channel_id=1, replica_groups=mesh['ta'=8,'ha'=32] {'ta'}, dimensions={0} | all-to-all | bytes 4194304 | tf_op jit(solution)/shard_map/all_to_all | solution.py:110
  149.9 1.2 copy.24
  151.0 2.8 %reshape.227 = bf16[1,32,2,16384]{3,2,0,1:T(2,128)(2,1)} reshape(bf16[1,32,2,8,2048]{4,3,2,1,0:T(8,128)(2,1)S(1)} %copy.24) | data formatting | bytes 4194304 | tf_op jit(solution)/shard_map/all_to_all | solution.py:110
  153.8 6.0 %all-to-all-start.1 = ((bf16[1,32,2,16384]{3,2,0,1:T(2,128)(2,1)}), bf16[1,32,2,16384]{3,2,0,1:T(2,128)(2,1)}, u32[]{:S(2)}, u32[]{:S(2)}) async-start(bf16[1,32,2,16384]{3,2,0,1:T(2,128)(2,1)} %reshape.227), calls=%async_computation.1 | async-start | bytes 4194304 | tf_op jit(solution)/shard_map/all_to_all | solution.py:109
  159.8 0.0 copy-done.5
  159.8 0.1 fusion.43
  159.9 0.1 reduce_window_sum.26
  159.9 0.0 copy-done.4
  160.0 0.3 reduce-window.9
  160.3 0.1 slice.57
  160.4 0.2 select_reduce_fusion
  160.5 0.5 compare_and_fusion.8
  161.1 0.1 slice_reduce_fusion
  161.2 0.1 fusion.44
  161.4 0.2 sine_convert_fusion
  161.5 0.9 negate_convert_fusion
  162.4 0.6 maximum_bitcast_fusion.4
  163.0 0.3 fusion.32
  163.3 0.7 fusion.48
  164.0 12.7 %psum.7 = f32[384]{0:T(512)S(1)} all-reduce(f32[384]{0:T(512)S(1)} %get-tuple-element.142), channel_id=1, replica_groups=mesh['ta'=8,'ha'=32] {'ta'}, use_global_device_ids=true, to_apply=%region_1.2 | all-reduce | flops 384 | bytes 3072 | tf_op jit(solution)/shard_map/psum | solution.py:118
  176.7 0.6 add_sqrt_fusion
  177.3 10.8 %all-to-all-done.1 = bf16[1,32,2,16384]{3,2,0,1:T(2,128)(2,1)} async-done(((bf16[1,32,2,16384]{3,2,0,1:T(2,128)(2,1)}), bf16[1,32,2,16384]{3,2,0,1:T(2,128)(2,1)}, u32[]{:S(2)}, u32[]{:S(2)}) %all-to-all-start.1) | async-done | bytes 2097184 | tf_op jit(solution)/shard_map/all_to_all | solution.py:109
  188.1 2.7 %reshape.167 = bf16[64,16384]{1,0:T(8,128)(2,1)S(1)} reshape(bf16[1,32,2,16384]{3,2,0,1:T(2,128)(2,1)} %all-to-all-done.1) | data formatting | bytes 4194304 | tf_op jit(solution)/shard_map/reshape | solution.py:116
  190.9 1.2 gather_fusion
  192.1 0.0 copy-start.6
  192.1 0.2 copy.26
  192.4 0.7 copy.20
  193.0 0.0 copy-done.6
  193.1 1.5 fusion.21
  194.6 0.0 copy-start.2
  194.6 0.0 copy-start.3
  194.6 0.6 fusion.17
  195.2 0.1 copy-done.2
  195.3 0.0 copy-done.3
  195.4 0.4 fusion.14
  195.8 0.2 fusion.20
  196.0 0.3 copy.35
  196.4 0.0 copy-done.1
  196.4 0.0 copy-done.7
  196.4 5.5 %while.14 = (s32[]{:T(128)}, f32[32,512]{1,0:T(8,128)S(1)}, bf16[32,8192]{1,0:T(8,128)(2,1)S(1)}, s32[512]{0:T(512)S(1)}, s32[512]{0:T(512)S(1)}, /*index=5*/s32[]{:T(128)}, s32[]{:T(128)}, s32[]{:T(128)}, s32[]{:T(128)}) while((s32[]{:T(128)}, f32[32,512]{1,0:T(8,128)S(1)}, bf16[32,8192]{1,0:T(8,128)(2,1)S(1)}, s32[512]{0:T(512)S(1)}, ...), condition=%wide.region_7.9_spmd.clone, body=%wide.region_6.8_spmd.clone.sunk | while | flops 35161096 | bytes 209053 | solution.py:78
  196.4 0.6 fusion.56
  197.1 0.6 fusion.56
  197.8 0.6 fusion.56
  198.5 0.6 fusion.56
  199.2 0.6 fusion.56
  199.9 0.6 fusion.56
  200.6 0.6 fusion.56
  201.3 0.6 fusion.56
  201.9 0.6 broadcast_divide_fusion
  (28 shorter events, 0.1 us)
Async XLA Ops:
  7.2 55.9 %copy-start = (bf16[300,384]{1,0:T(8,128)(2,1)S(1)}, bf16[300,384]{1,0:T(8,128)(2,1)}, u32[]{:S(2)}) copy-start(bf16[300,384]{1,0:T(8,128)(2,1)} %param.11) | copy-start | bytes 691204
  7.2 55.9 %all-gather.2.cloned.1.call-start = ((), (), s32[]{:S(2)}) async-start(), calls=%async_computation.2 | async-start | bytes 1622016 | tf_op jit(solution)/shard_map/all_gather | solution.py:99
  153.8 6.0 %copy-start.5 = (s32[32]{0:T(128)S(1)}, s32[32]{0:T(128)}, u32[]{:S(2)}) copy-start(s32[32]{0:T(128)} %param.14) | copy-start | bytes 388
  153.8 6.1 %copy-start.4 = (s32[512]{0:T(512)S(1)}, s32[512]{0:T(512)}, u32[]{:S(2)}) copy-start(s32[512]{0:T(512)} %param.15) | copy-start | bytes 6148
  153.8 34.3 %all-to-all-start.1 = ((bf16[1,32,2,16384]{3,2,0,1:T(2,128)(2,1)}), bf16[1,32,2,16384]{3,2,0,1:T(2,128)(2,1)}, u32[]{:S(2)}, u32[]{:S(2)}) async-start(bf16[1,32,2,16384]{3,2,0,1:T(2,128)(2,1)} %reshape.227), calls=%async_computation.1 | async-start | bytes 4194304 | tf_op jit(solution)/shard_map/all_to_all | solution.py:109
  192.1 0.9 copy-start.6
  194.6 0.8 copy-start.2
  194.6 0.8 copy-start.3
  195.3 1.0 copy-start.1
  195.3 1.0 copy-start.7
  195.4 1.0 copy-start.8
Sparse Core Ops, SparseCore 0:
  10.6 52.4 all-gather.1
where the time goes:
time: 210 us; the launch traced here: 209 us
  blocking collectives  70.6 us (34%)
  waiting for transfers between devices  64.8 us (31%)
  local copies, waits for them, and re-layouts  30.7 us (15%)
  between operations  14.3 us (7%)
  other arithmetic  13 us (6%)
  matrix products  9.66 us (5%)
  starting transfers between devices  6.01 us (3%)
    all_to_all x1, blocking collectives, shards(): lax.all_to_all(sending, 'ta', split_axis=0, concat_axis=3, tiled=True)  57.9 us
    all_gather x1, waiting for transfers between devices, shards(): lax.all_gather(mode_record, 'ha', axis=1, tiled=True)  53.3 us
    psum x1, blocking collectives, shards(): energy = lax.psum(jnp.sum(stress * stress, axis=1), 'ta')  12.7 us
    all_to_all x1, waiting for transfers between devices, shards(): lax.all_to_all(lax.all_to_all(sending, 'ta', split_axis=0, concat_axis=3,...  10.8 us
    gather x3, local copies, waits for them, and re-layouts, shards(): jnp.take(stress, map_elem[term_index], axis=0)  10.8 us
    convert_element_type x1, other arithmetic, shards(): slot_rows.astype(jnp.bfloat16)  6.9 us
    all_to_all x1, starting transfers between devices, shards(): lax.all_to_all(lax.all_to_all(sending, 'ta', split_axis=0, concat_axis=3,...  5.97 us
    dot_general x8, matrix products, add_block(): jnp.dot(part_power, member, preferred_element_type=jnp.float32)  5.19 us
  transfers between devices with their start and end apart: 2, of which 2 were waited for; matrix products, arithmetic and copies ran while one was open for 3% of the time, Pallas kernels for 0%

commit v1 on v0

v1 whole, which is shorter than its diff:
```python
import jax
import jax.numpy as jnp
import numpy as np
from jax import lax
from jax.experimental import pallas as pl
from jax.experimental.pallas import tpu as pltpu
from jax.sharding import PartitionSpec as P

DFT_LEN = 128
NB = 512
K_EXT = 4
HS_DEV = 32
NT = 16384
MODES = 300
E_DEV = 384
FOLD = 160
KPAD = 320
HALF = 64

epsilon = 1e-06
MESH = pl.DeviceIdType.MESH
PLANES = (0, 1, 7, 2, 6, 3, 5, 4)
PLANE_AT = {dz: i for i, dz in enumerate(PLANES)}


def tables():
    import ml_dtypes

    pos = np.arange(DFT_LEN)
    turn = np.float32(2.0 * np.pi / DFT_LEN)
    first = (pos[:, None] * pos[None, :] % DFT_LEN).astype(np.float32) * turn
    first_table = np.concatenate([np.cos(first), -np.sin(first)], axis=0)
    fine = (pos[:, None] * pos[None, :]).astype(np.float32) * np.float32(2.0 * np.pi / NT)
    twiddle = []
    for half in range(2):
        part = fine[:, half * HALF : (half + 1) * HALF]
        part = np.concatenate([part, part], axis=1)
        twiddle += [np.cos(part), np.sin(part)]
    second = np.zeros((4, 2, HALF, 2, 2, HALF), np.float32)
    for half in range(2):
        angles = first[half * HALF : (half + 1) * HALF, :HALF]
        c, s = np.cos(angles), np.sin(angles)
        for hh in range(2):
            second[2 * half, hh, :, 0, hh] = c
            second[2 * half, hh, :, 1, hh] = -s
            second[2 * half + 1, hh, :, 0, hh] = s
            second[2 * half + 1, hh, :, 1, hh] = c
    return (
        first_table.astype(ml_dtypes.bfloat16),
        np.stack(twiddle).astype(np.float32),
        second.reshape(512, 256).astype(ml_dtypes.bfloat16),
    )


def kernel(
    rec_ref, shapes_ref, elem_ref, coef_ref, owner_ref, bins_ref, first_ref, turn_ref, second_ref,
    band_ref, energy_ref,
    pad_rec, pad_shapes, shapes_out, shapes_in, shapes_t,
    c_rows, c_out, c_in, c_flat, hot_mine, hot_in,
    gathered, wide, folded, sending, arrived,
    member, power, power_rows, table, e_acc, e_mine, e_in, e_sum, e_all,
    shp_ss, shp_rs, c_ss, c_rs, hot_ss, hot_rs, g_ss, g_rs, s_ss, s_rs, e1_ss, e1_rs, e2_ss, e2_rs,
):
    f32, bf16, i32 = jnp.float32, jnp.bfloat16, jnp.int32
    z = lax.axis_index("ta")
    ha = lax.axis_index("ha")
    core = lax.rem(ha, 2)
    x = lax.div(ha, 8)
    y = lax.rem(lax.div(ha, 2), 4)
    u = jnp.where(core == 0, x, y)
    v = jnp.where(core == 0, y, x)
    z_half, z_odd = lax.div(z, 2), lax.rem(z, 2)

    def at(px, py, pz, pc):
        return (pz, (px * 4 + py) * 2 + pc)

    def line(plane_core, pu, pv, pz, pc):
        return at(
            jnp.where(plane_core == 0, pu, pv), jnp.where(plane_core == 0, pv, pu), pz, pc
        )

    def send(src, dst, ss, rs, device):
        copy = pltpu.make_async_remote_copy(
            src_ref=src, dst_ref=dst, send_sem=ss, recv_sem=rs, device_id=device, device_id_type=MESH
        )
        copy.start()
        return copy

    def wait(ref, sem):
        pltpu.make_async_copy(ref, ref, sem).wait()

    barrier = pltpu.get_barrier_semaphore()

    def greet_plane(o, _):
        pl.semaphore_signal(
            barrier, inc=1, device_id=(z, lax.rem(ha + o, 32)), device_id_type=MESH
        )
        return 0

    def greet_line(o, _):
        pl.semaphore_signal(barrier, inc=1, device_id=(lax.rem(z + o, 8), ha), device_id_type=MESH)
        return 0

    lax.fori_loop(1, 32, greet_plane, 0)
    lax.fori_loop(1, 8, greet_line, 0)

    lane128 = lax.broadcasted_iota(i32, (1, 128), 1)
    left = lane128 < HALF

    def swap(tile):
        return pltpu.roll(tile, HALF, 1)

    pad_rec[...] = jnp.zeros_like(pad_rec)
    pad_rec[0:HALF, 0:MODES] = rec_ref[...].astype(f32)
    turned = pad_rec[...].T
    gathered[0] = (turned[0:FOLD] + swap(turned[FOLD : 2 * FOLD])).astype(bf16)

    shapes_out[MODES - 12 : 304, :] = jnp.zeros((16, E_DEV), bf16)
    shapes_out[0:MODES, :] = shapes_ref[...]
    slots = pl.ds(pl.multiple_of(z_half * 128, 128), 128)
    elems = elem_ref[:, slots]
    coefs = coef_ref[:, slots]
    elem_ids = lax.broadcasted_iota(i32, (E_DEV, 128), 0)
    hot = jnp.zeros((304, 128), f32)
    for k in range(K_EXT):
        pick = (elem_ids == elems[k : k + 1, :]).astype(f32).astype(bf16)
        hot = hot + coefs[k : k + 1, :] * jnp.dot(
            shapes_out[...], pick, preferred_element_type=f32
        )
    c_rows[...] = jnp.concatenate([hot, jnp.zeros((80, 128), f32)], axis=0).T

    def spread(i, _):
        c_out[i] = c_rows[pl.ds(z_odd * HALF + i, 1), :]
        return 0

    lax.fori_loop(0, 64, spread, 0)

    col = lax.broadcasted_iota(i32, (128, 128), 1)
    row = lax.broadcasted_iota(i32, (128, 128), 0)
    source, place, dv = lax.div(col, 32), lax.div(lax.rem(col, 32), 4), lax.rem(col, 4)
    dz = jnp.zeros_like(col)
    for i, value in enumerate(PLANES):
        dz = jnp.where(place == i, value, dz)
    zz = lax.rem(z + dz, 8)
    a_even = 16 * zz + 4 * lax.rem(x + source, 4) + lax.rem(y + dv, 4)
    a_odd = 16 * zz + 4 * lax.rem(x + dv, 4) + lax.rem(y + source, 4)
    for half, a_of in enumerate((a_even, a_odd)):
        order = (row == a_of).astype(f32).astype(bf16)
        table[half] = jnp.dot(first_ref[...], order, preferred_element_type=f32).astype(bf16)

    pl.semaphore_wait(barrier, 38)

    copies = []
    g_count = [0]

    def g_send(q, j, rows, dq, dj, device):
        n = g_count[0]
        g_count[0] += 1
        copies.append(
            send(
                gathered.at[q * 4 + j], gathered.at[dq * 4 + dj], g_ss.at[n],
                g_rs.at[dq * 4 + dj], device,
            )
        )

    up, down = lax.rem(z + 1, 8), lax.rem(z + 7, 8)

    def z_send(k, j, go_up):
        here = (8 - k) % 8 if go_up else k
        there = (8 - k - 1) % 8 if go_up else k + 1
        g_send(
            PLANE_AT[here], j, None, PLANE_AT[there], j,
            line(core, u, v, up if go_up else down, core),
        )

    def g_wait(q, j):
        wait(gathered.at[q * 4 + j], g_rs.at[q * 4 + j])

    for j in (1, 3, 2):
        g_send(0, 0, None, 0, j, line(core, u, lax.rem(v + 4 - j, 4), z, core))
    z_send(0, 0, True)
    z_send(0, 0, False)

    def c_send(o, _):
        to = lax.rem(ha + o, 32)
        pltpu.make_async_remote_copy(
            src_ref=c_out.at[pl.ds(2 * to, 2)], dst_ref=c_in.at[pl.ds(2 * (32 - o), 2)],
            send_sem=c_ss, recv_sem=c_rs, device_id=(z, to), device_id_type=MESH,
        ).start()
        return 0

    lax.fori_loop(1, 32, c_send, 0)
    c_in[0] = c_out[2 * ha]
    c_in[1] = c_out[2 * ha + 1]

    owns = core == z_odd
    shp_to = [
        line(0, lax.rem(x + 4 - z_half, 4), y, z, 0),
        line(1, lax.rem(y + 4 - z_half, 4), x, z, 1),
    ]

    def shape_copies(act):
        for cc in range(2):
            own_work = jnp.logical_and(z_half == 0, core == cc)

            @pl.when(jnp.logical_and(owns, jnp.logical_not(own_work)))
            def _():
                act(
                    pltpu.make_async_remote_copy(
                        src_ref=shapes_out, dst_ref=shapes_in, send_sem=shp_ss.at[cc],
                        recv_sem=shp_rs, device_id=shp_to[cc], device_id_type=MESH,
                    )
                )

    shape_copies(lambda copy: copy.start())
    local_shapes = jnp.logical_and(owns, z_half == 0)

    @pl.when(local_shapes)
    def _():
        shapes_in[...] = shapes_out[...]

    for j in (1, 3, 2):
        g_wait(0, j)
        z_send(0, j, True)
        z_send(0, j, False)

    bins = bins_ref[...].astype(f32)
    before = (
        lax.broadcasted_iota(i32, (NB, NB), 0) < lax.broadcasted_iota(i32, (NB, NB), 1)
    ).astype(f32).astype(bf16)
    starts = jnp.dot(
        jnp.broadcast_to(bins, (8, NB)).astype(bf16), before, preferred_element_type=f32
    )[0:1]
    starts_i = starts.astype(i32)
    ends_i = (starts + bins).astype(i32)

    def member_block(i, _):
        rows = lax.broadcasted_iota(i32, (256, 1), 0)
        bin_ids = i * 4 + lax.div(rows, HALF) + DFT_LEN * lax.rem(rows, HALF)
        inside = jnp.logical_and(bin_ids >= starts_i, bin_ids < ends_i)
        member[pl.ds(pl.multiple_of(i * 256, 256), 256), :] = inside.astype(f32).astype(bf16)
        return 0

    lax.fori_loop(0, 16, member_block, 0)

    def step(k):
        for j in (0, 1, 3, 2):
            for go_up in (True, False):
                here = (8 - k) % 8 if go_up else k
                g_wait(PLANE_AT[here], j)
                if k < 3 or (j in (0, 1)) == go_up:
                    z_send(k, j, go_up)

    step(1)

    wait(c_in.at[pl.ds(2, 62)], c_rs)

    def flatten(i, _):
        c_flat[pl.ds(i, 1), :] = c_in[i]
        return 0

    lax.fori_loop(0, 64, flatten, 0)
    owner_row = owner_ref[...]
    r32 = lax.broadcasted_iota(i32, (32, 32), 0)
    c32 = lax.broadcasted_iota(i32, (32, 32), 1)
    owners = jnp.broadcast_to(owner_row, (32, 32))
    owner_col = jnp.sum(jnp.where(r32 == c32, owners, 0), axis=1, keepdims=True)
    rank = jnp.sum(
        jnp.logical_and(owners == owner_col, c32 < r32).astype(i32), axis=1, keepdims=True
    )
    slot = lax.broadcasted_iota(i32, (32, 64), 1)
    region = lax.rem(ha + lax.div(slot, 2), 32)
    chosen = jnp.logical_and(region == owner_col, lax.rem(slot, 2) == rank)
    chosen = chosen.astype(f32).astype(bf16)
    flat = c_flat[...]
    high = flat.astype(bf16)
    low = (flat - high.astype(f32)).astype(bf16)
    high = jnp.dot(chosen, high, preferred_element_type=f32)
    low = jnp.dot(chosen, low, preferred_element_type=f32)
    hot_mine[...] = jnp.concatenate(
        [high[:, 0:256], high[:, 256:384] + swap(low[:, 256:384]), low[:, 0:256]], axis=1
    ).astype(bf16)
    hot_in[core] = hot_mine[...]
    for du in range(1, 4):
        for cc in range(2):
            here_u, here_v = (x, y) if cc == 0 else (y, x)
            copies.append(
                send(
                    hot_mine, hot_in.at[du * 2 + core], hot_ss.at[du * 2 + cc],
                    hot_rs.at[du * 2 + core], line(cc, lax.rem(here_u + 4 - du, 4), here_v, z, cc),
                )
            )
    copies.append(
        send(hot_mine, hot_in.at[core], hot_ss.at[0], hot_rs.at[core], at(x, y, z, 1 - core))
    )

    lax.fori_loop(16, 32, member_block, 0)
    step(2)

    @pl.when(jnp.logical_not(local_shapes))
    def _():
        wait(shapes_in, shp_rs)

    pad_shapes[0:304, :] = shapes_in[...].astype(f32)
    pad_shapes[304:384, :] = jnp.zeros((80, E_DEV), f32)
    shapes_t[...] = pad_shapes[...].T.astype(bf16)
    e_acc[...] = jnp.zeros_like(e_acc)

    def unfold(q):
        parts = []
        for pair in range(2):
            even = gathered[q * 4 + 2 * pair].astype(f32)
            odd = gathered[q * 4 + 2 * pair + 1].astype(f32)
            parts.append(
                (
                    jnp.where(left, even, swap(odd)).astype(bf16),
                    jnp.where(left, swap(even), odd).astype(bf16),
                )
            )
        first = jnp.concatenate([parts[0][0], parts[1][0]], axis=1)
        last = jnp.concatenate([parts[0][1], parts[1][1]], axis=1)
        wide[0:160, :] = first
        wide[160:320, :] = last
        wide[320:384, :] = last[96:160]
        wide[384:544, :] = first
        wide[544:640, :] = last[0:96]

    def energies():
        stress = jnp.dot(shapes_t[...], wide[0:384, :], preferred_element_type=f32)
        squares = stress * stress
        e_acc[...] += squares[:, 0:128] + squares[:, 128:256]

    def series(q):
        out = jnp.dot(
            hot_in[...].reshape(256, 640), wide[...], preferred_element_type=f32
        ).reshape(8, 2, 16, 256)
        for pair in range(2):
            lanes = slice(pair * 128, pair * 128 + 128)
            top = out[:, 0, :, lanes].reshape(128, 128)
            low_half = out[:, 1, :, lanes].reshape(128, 128)
            for n, tile in enumerate(
                (
                    jnp.where(left, top, swap(low_half)),
                    jnp.where(left, swap(top), low_half),
                )
            ):
                folded[pl.ds((q % 4) * 4 + pair * 2 + n, 128, stride=16), :] = tile

    def s_send(piece):
        sending[piece] = folded[...].astype(bf16).reshape(8, 16, 16, 128)
        arrived[core, 0, piece] = sending[piece, core]
        for du in range(1, 4):
            for cc in range(2):
                n = du * 2 + cc
                copies.append(
                    send(
                        sending.at[piece, n], arrived.at[core, (4 - du) % 4, piece],
                        s_ss.at[piece, n], s_rs.at[core, (4 - du) % 4, piece],
                        line(core, lax.rem(u + du, 4), v, z, cc),
                    )
                )
        copies.append(
            send(
                sending.at[piece, 1 - core], arrived.at[core, 0, piece], s_ss.at[piece, 0],
                s_rs.at[core, 0, piece], at(x, y, z, 1 - core),
            )
        )

    for du in range(1, 4):
        for cc in range(2):
            wait(hot_in.at[du * 2 + cc], hot_rs.at[du * 2 + cc])
    wait(hot_in.at[1 - core], hot_rs.at[1 - core])

    for q in range(4):
        unfold(q)
        series(q)
        energies()
    s_send(0)
    step(3)
    for q in range(4, 7):
        unfold(q)
        series(q)
        energies()
    for j in range(4):
        g_wait(7, j)
    unfold(7)
    series(7)
    s_send(1)
    energies()

    e_mine[0] = jnp.sum(e_acc[...].T, axis=0, keepdims=True)
    e_local = jnp.logical_and(z_half == 0, core == z_odd)
    e_to = line(core, lax.rem(u + z_half, 4), v, z, z_odd)

    def e_first(act):
        @pl.when(jnp.logical_not(e_local))
        def _():
            act(
                pltpu.make_async_remote_copy(
                    src_ref=e_mine, dst_ref=e_in.at[pl.ds(core, 1)], send_sem=e1_ss,
                    recv_sem=e1_rs.at[core], device_id=e_to, device_id_type=MESH,
                )
            )

    e_first(lambda copy: copy.start())

    @pl.when(e_local)
    def _():
        e_in[core] = e_mine[0]

    def e_second(act):
        @pl.when(owns)
        def _():
            def one(o, _):
                act(
                    pltpu.make_async_remote_copy(
                        src_ref=e_sum, dst_ref=e_all.at[pl.ds(z_half, 1)], send_sem=e2_ss.at[o],
                        recv_sem=e2_rs.at[z_half], device_id=(lax.rem(z + o, 8), ha),
                        device_id_type=MESH,
                    )
                )
                return 0

            lax.fori_loop(1, 8, one, 0)

    @pl.when(owns)
    def _():
        for cc in range(2):

            @pl.when(jnp.logical_not(jnp.logical_and(z_half == 0, core == cc)))
            def _():
                wait(e_in.at[pl.ds(cc, 1)], e1_rs.at[cc])

        e_sum[0] = e_in[0] + e_in[1]
        e_all[z_half] = e_sum[0]

    e_second(lambda copy: copy.start())

    for piece in range(2):
        for half in range(2):
            for du in range(1, 4):
                wait(arrived.at[half, du, piece], s_rs.at[half, du, piece])
        wait(arrived.at[1 - core, 0, piece], s_rs.at[1 - core, 0, piece])

    def spectrum(pp, _):
        ones = []
        for half in range(2):
            tiles = []
            for n in range(2):
                tiles.append(
                    jnp.concatenate(
                        [
                            arrived[half, i, piece, 2 * pp + n]
                            for i in range(4)
                            for piece in range(2)
                        ],
                        axis=0,
                    )
                )
            one = jnp.dot(
                table[half], jnp.concatenate(tiles, axis=1), preferred_element_type=f32
            )
            ones.append(one)
        for n in range(2):
            lanes = slice(n * 128, n * 128 + 128)
            blocks = []
            for half in range(2):
                real, imag = ones[half][0:128, lanes], ones[half][128:256, lanes]
                c, s = turn_ref[2 * half], turn_ref[2 * half + 1]
                blocks += [(real * c + imag * s).astype(bf16), (imag * c - real * s).astype(bf16)]
            out = jnp.dot(
                jnp.concatenate(blocks, axis=1), second_ref[...], preferred_element_type=f32
            )
            real, imag = out[:, 0:128], out[:, 128:256]
            power[pl.ds(2 * pp + n, 128, stride=16), :] = real * real + imag * imag
        return 0

    lax.fori_loop(0, 8, spectrum, 0)

    for kb in range(32):
        tiles = []
        for pair in range(2):
            base = (kb * 4 + pair * 2) * 16
            even, odd = power[base : base + 16, :], power[base + 16 : base + 32, :]
            tiles.append(
                jnp.concatenate(
                    [jnp.where(left, even, swap(odd)), jnp.where(left, swap(even), odd)], axis=0
                )
            )
        power_rows[:, kb * 256 : kb * 256 + 256] = jnp.concatenate(tiles, axis=1).astype(bf16)
    band_ref[...] = jnp.dot(power_rows[...], member[...], preferred_element_type=f32)

    for i in range(4):

        @pl.when(jnp.logical_not(jnp.logical_and(owns, z_half == i)))
        def _():
            wait(e_all.at[pl.ds(i, 1)], e2_rs.at[i])

    energy_ref[...] = (e_all[0] + e_all[1]) + (e_all[2] + e_all[3])

    for copy in copies:
        copy.wait_send()
    wait(c_out.at[pl.ds(2, 62)], c_ss)
    shape_copies(lambda copy: copy.wait_send())
    e_first(lambda copy: copy.wait_send())
    e_second(lambda copy: copy.wait_send())


def shards(mode_record, mode_shapes, map_elem, map_coef, hot_owner, band_bins):
    f32, bf16 = jnp.float32, jnp.bfloat16
    first, turn, second = tables()
    vmem, dma = pltpu.VMEM, pltpu.SemaphoreType.DMA
    scratch = [
        vmem((128, 384), f32),
        vmem((384, 384), f32),
        vmem((304, 384), bf16),
        vmem((304, 384), bf16),
        vmem((384, 384), bf16),
        vmem((128, 384), f32),
        vmem((64, 1, 384), f32),
        vmem((64, 1, 384), f32),
        vmem((64, 384), f32),
        vmem((32, 640), bf16),
        vmem((8, 32, 640), bf16),
        vmem((32, FOLD, 128), bf16),
        vmem((640, 256), bf16),
        vmem((2048, 128), f32),
        vmem((2, 8, 16, 16, 128), bf16),
        vmem((2, 4, 2, 16, 16, 128), bf16),
        vmem((NT // 2, NB), bf16),
        vmem((2048, 128), f32),
        vmem((32, NT // 2), bf16),
        vmem((2, 256, 128), bf16),
        vmem((384, 128), f32),
        vmem((1, 1, 384), f32),
        vmem((2, 1, 384), f32),
        vmem((1, 1, 384), f32),
        vmem((4, 1, 384), f32),
        dma((2,)), dma, dma, dma, dma((8,)), dma((8,)), dma((31,)), dma((32,)),
        dma((2, 8)), dma((2, 4, 2)), dma, dma((2,)), dma((8,)), dma((4,)),
    ]
    whole = pl.BlockSpec(memory_space=pltpu.VMEM)
    sums, energy = pl.pallas_call(
        kernel,
        out_shape=(
            jax.ShapeDtypeStruct((HS_DEV, NB), f32),
            jax.ShapeDtypeStruct((1, E_DEV), f32),
        ),
        in_specs=[whole] * 9,
        out_specs=(whole, whole),
        scratch_shapes=scratch,
        compiler_params=pltpu.CompilerParams(
            collective_id=0, has_side_effects=True, vmem_limit_bytes=48 * 2**20
        ),
        name="whipping",
    )(
        mode_record.T, mode_shapes, map_elem, map_coef, hot_owner.reshape(1, HS_DEV),
        band_bins.reshape(1, NB), jnp.asarray(first), jnp.asarray(turn), jnp.asarray(second),
    )
    elem_rms = jnp.sqrt(energy.reshape(E_DEV) / NT + epsilon)
    band_power = sums / (NT * band_bins.astype(f32))[None, :]
    return (elem_rms, band_power)


def solution(mesh):
    in_specs = (
        P(None, ("ta", "ha")),
        P(None, "ha"),
        P(None, "ha"),
        P(None, "ha"),
        P(("ta", "ha")),
        P(),
    )
    out_specs = (P("ha"), P(("ta", "ha"), None))
    return jax.shard_map(shards, mesh=mesh, in_specs=in_specs, out_specs=out_specs, check_vma=False)
```

time: 210 us -> 51.7 us (0.25)
  blocking collectives: 70.6 us -> 0 us
  waiting for transfers between devices: 64.8 us -> 0 us
  Pallas kernels: 0 us -> 42.9 us
  local copies, waits for them, and re-layouts: 30.7 us -> 6.54 us
  between operations: 14.3 us -> 0.67 us
  other arithmetic: 13 us -> 1.25 us
  matrix products: 9.66 us -> 0 us
  starting transfers between devices: 6.01 us -> 0 us
    all_to_all x1 -> x0, blocking collectives: 57.9 us -> none  [shards(): lax.all_to_all(sending, 'ta', split_axis=0, concat_axis=3, tiled=True)]
    all_gather x1 -> x0, waiting for transfers between devices: 53.3 us -> none  [shards(): lax.all_gather(mode_record, 'ha', axis=1, tiled=True)]
    pallas_call x0 -> x1, Pallas kernels: none -> 42.9 us  [shards(): pl.pallas_call(kernel, out_shape=(jax.ShapeDtypeStruct((HS_DEV, NB), f32)...]
    gather x6 -> x0, local copies, waits for them, and re-layouts: 16.3 us -> none  [the longest x3 10.8 us: shards(): jnp.take(stress, map_elem[term_index], axis=0)]
    psum x1 -> x0, blocking collectives: 12.7 us -> none  [shards(): energy = lax.psum(jnp.sum(stress * stress, axis=1), 'ta')]
    all_to_all x1 -> x0, waiting for transfers between devices: 10.8 us -> none  [shards(): lax.all_to_all(lax.all_to_all(sending, 'ta', split_axis=0, concat_axis=3,...]
    dot_general x11 -> x0, matrix products: 9.66 us -> none  [the longest x8 5.19 us: add_block(): jnp.dot(part_power, member, preferred_element_type=jnp.float32)]
    reshape x3 -> x0, local copies, waits for them, and re-layouts: 7.86 us -> none  [the longest x2 5.12 us: shards(): slot_rows.astype(jnp.bfloat16)]
  transfers between devices with their start and end apart: 2 -> 0, of which waited for: 2 -> 0; matrix products, arithmetic and copies ran while one was open for 3% -> 0% of each run, Pallas kernels for 0% -> 0%
where the time goes in v1:
time: 51.7 us; the launch traced here: 51.3 us
  Pallas kernels  42.9 us (83%)
  local copies, waits for them, and re-layouts  6.54 us (13%)
  other arithmetic  1.25 us (2%)
  between operations  0.67 us (1%)
    pallas_call x1, Pallas kernels, shards(): pl.pallas_call(kernel, out_shape=(jax.ShapeDtypeStruct((HS_DEV, NB), f32)...  42.9 us
    unnamed x18, local copies, waits for them, and re-layouts  6.54 us

profile of v1, /device:TPU:1, one launch (start us, length us, event | category | flops | bytes accessed | tf_op | source)
XLA Modules:
  0.0 51.3 jit_solution(9167976476514946067)
XLA Ops:
  0.6 0.0 copy-start.7
  0.6 0.0 copy-start.8
  0.7 0.7 %copy-done.7 = s32[512]{0:T(512)S(1)} copy-done((s32[512]{0:T(512)S(1)}, s32[512]{0:T(512)}, u32[]{:S(2)}) %copy-start.7) | copy-done | bytes 2072
  1.3 0.0 copy-done.8
  1.3 0.0 copy-start
  1.3 0.9 %copy-done = f32[4,128,128]{2,1,0:T(8,128)S(1)} copy-done((f32[4,128,128]{2,1,0:T(8,128)S(1)}, f32[4,128,128]{2,1,0:T(8,128)}, u32[]{:S(2)}) %copy-start) | copy-done | bytes 262168
  2.3 0.0 copy-start.1
  2.3 0.9 %copy-done.1 = bf16[512,256]{1,0:T(8,128)(2,1)S(1)} copy-done((bf16[512,256]{1,0:T(8,128)(2,1)S(1)}, bf16[512,256]{1,0:T(8,128)(2,1)}, u32[]{:S(2)}) %copy-start.1) | copy-done | bytes 262168
  3.2 0.0 copy-start.2
  3.2 0.9 %copy-done.2 = bf16[300,384]{1,0:T(8,128)(2,1)S(1)} copy-done((bf16[300,384]{1,0:T(8,128)(2,1)S(1)}, bf16[300,384]{1,0:T(8,128)(2,1)}, u32[]{:S(2)}) %copy-start.2) | copy-done | bytes 230424
  4.2 0.0 copy-start.3
  4.2 0.8 %copy-done.3 = bf16[256,128]{1,0:T(8,128)(2,1)S(1)} copy-done((bf16[256,128]{1,0:T(8,128)(2,1)S(1)}, bf16[256,128]{1,0:T(8,128)(2,1)}, u32[]{:S(2)}) %copy-start.3) | copy-done | bytes 65560
  5.0 0.0 copy-start.4
  5.0 0.8 %copy-done.4 = bf16[300,64]{0,1:T(8,128)(2,1)S(1)} copy-done((bf16[300,64]{0,1:T(8,128)(2,1)S(1)}, bf16[300,64]{0,1:T(8,128)(2,1)}, u32[]{:S(2)}) %copy-start.4) | copy-done | bytes 38424
  5.8 0.0 copy-start.5
  5.8 0.7 %copy-done.5 = s32[4,512]{1,0:T(4,128)S(1)} copy-done((s32[4,512]{1,0:T(4,128)S(1)}, s32[4,512]{1,0:T(4,128)}, u32[]{:S(2)}) %copy-start.5) | copy-done | bytes 8216
  6.5 0.0 copy-start.6
  6.5 0.7 %copy-done.6 = f32[4,512]{1,0:T(4,128)S(1)} copy-done((f32[4,512]{1,0:T(4,128)S(1)}, f32[4,512]{1,0:T(4,128)}, u32[]{:S(2)}) %copy-start.6) | copy-done | bytes 8216
  7.2 42.9 %whipping.1 = (f32[32,512]{1,0:T(8,128)S(1)}, f32[1,384]{1,0:T(1,128)S(1)}) custom-call(bf16[64,300]{1,0:T(8,128)(2,1)S(1)} %bitcast.3, bf16[300,384]{1,0:T(8,128)(2,1)S(1)} %copy-done.2, s32[4,512]{1,0:T(4,128)S(1)} %copy-done.5, f32[4,512]{1,0:T(4,128)S(1)} %copy-done.6, s32[1,32]{1,0:T(1,128)S(1)} %bitcast.5, s32[1,512]{1,0:T(1,128)S(1)} %bitcast.4, ...), custom_call_target="tpu_custom_call" | custom-call | tf_op jit(solution)/shard_map/whipping/pallas_call | solution.py:543
  50.1 0.6 %broadcast_divide_fusion = f32[32,512]{1,0:T(8,128)} fusion(f32[32,512]{1,0:T(8,128)S(1)} %get-tuple-element.5, f32[512]{0:T(512)S(1)} %convert_multiply_fusion), kind=kLoop, calls=%fused_computation | loop fusion | flops 16384 | bytes 133120 | tf_op jit(solution)/shard_map/div | solution.py:561
  50.7 0.6 %sqrt_reduce_fusion = f32[384]{0:T(512)} fusion(f32[1,384]{1,0:T(1,128)S(1)} %get-tuple-element.4), kind=kLoop, calls=%fused_computation.2 | loop fusion | flops 768 | bytes 3072 | tf_op jit(solution)/shard_map/sqrt | solution.py:560
  (1 shorter events, 0.0 us)
Async XLA Ops:
  0.6 0.7 %copy-start.7 = (s32[512]{0:T(512)S(1)}, s32[512]{0:T(512)}, u32[]{:S(2)}) copy-start(s32[512]{0:T(512)} %param.14) | copy-start | bytes 6148
  0.6 0.7 %copy-start.8 = (s32[32]{0:T(128)S(1)}, s32[32]{0:T(128)}, u32[]{:S(2)}) copy-start(s32[32]{0:T(128)} %param.13) | copy-start | bytes 388
  1.3 1.0 %copy-start = (f32[4,128,128]{2,1,0:T(8,128)S(1)}, f32[4,128,128]{2,1,0:T(8,128)}, u32[]{:S(2)}) copy-start(f32[4,128,128]{2,1,0:T(8,128)} %constant.14.clone.turn_ref) | copy-start | bytes 786436
  2.3 0.9 %copy-start.1 = (bf16[512,256]{1,0:T(8,128)(2,1)S(1)}, bf16[512,256]{1,0:T(8,128)(2,1)}, u32[]{:S(2)}) copy-start(bf16[512,256]{1,0:T(8,128)(2,1)} %constant.15.clone.second_ref) | copy-start | bytes 786436
  3.2 0.9 %copy-start.2 = (bf16[300,384]{1,0:T(8,128)(2,1)S(1)}, bf16[300,384]{1,0:T(8,128)(2,1)}, u32[]{:S(2)}) copy-start(bf16[300,384]{1,0:T(8,128)(2,1)} %shapes_ref.1) | copy-start | bytes 691204
  4.2 0.8 %copy-start.3 = (bf16[256,128]{1,0:T(8,128)(2,1)S(1)}, bf16[256,128]{1,0:T(8,128)(2,1)}, u32[]{:S(2)}) copy-start(bf16[256,128]{1,0:T(8,128)(2,1)} %constant.13.clone.first_ref) | copy-start | bytes 196612
  5.0 0.8 %copy-start.4 = (bf16[300,64]{0,1:T(8,128)(2,1)S(1)}, bf16[300,64]{0,1:T(8,128)(2,1)}, u32[]{:S(2)}) copy-start(bf16[300,64]{0,1:T(8,128)(2,1)} %param.9) | copy-start | bytes 115204
  5.8 0.7 %copy-start.5 = (s32[4,512]{1,0:T(4,128)S(1)}, s32[4,512]{1,0:T(4,128)}, u32[]{:S(2)}) copy-start(s32[4,512]{1,0:T(4,128)} %elem_ref.1) | copy-start | bytes 24580
  6.5 0.7 %copy-start.6 = (f32[4,512]{1,0:T(4,128)S(1)}, f32[4,512]{1,0:T(4,128)}, u32[]{:S(2)}) copy-start(f32[4,512]{1,0:T(4,128)} %coef_ref.1) | copy-start | bytes 24580

commit v2 on v1

--- a/solution.py
+++ b/solution.py
@@ -48,18 +48,20 @@
     return (
         first_table.astype(ml_dtypes.bfloat16),
         np.stack(twiddle).astype(np.float32),
-        second.reshape(512, 256).astype(ml_dtypes.bfloat16),
+        second.reshape(512, 256).astype(ml_dtypes.bfloat16).astype(np.float32),
     )
 
 
 def kernel(
+    rec_hbm, shapes_hbm, elem_hbm, coef_hbm, owner_hbm, bins_hbm, first_hbm, turn_hbm, second_hbm,
+    band_ref, energy_ref,
     rec_ref, shapes_ref, elem_ref, coef_ref, owner_ref, bins_ref, first_ref, turn_ref, second_ref,
-    band_ref, energy_ref,
     pad_rec, pad_shapes, shapes_out, shapes_in, shapes_t,
     c_rows, c_out, c_in, c_flat, hot_mine, hot_in,
     gathered, wide, folded, sending, arrived,
-    member, power, power_rows, table, e_acc, e_mine, e_in, e_sum, e_all,
-    shp_ss, shp_rs, c_ss, c_rs, hot_ss, hot_rs, g_ss, g_rs, s_ss, s_rs, e1_ss, e1_rs, e2_ss, e2_rs,
+    member, twiddled, power, table, e_acc, e_mine, e_in, e_sum, e_all,
+    shp_ss, shp_rs, c_ss, c_rs, hot_ss, hot_rs, g_ss, g_rs, z_ss, far_rs, s_ss, s_rs, e1_ss, e1_rs, e2_ss, e2_rs,
+    in_sem,
 ):
     f32, bf16, i32 = jnp.float32, jnp.bfloat16, jnp.int32
     z = lax.axis_index("ta")
@@ -89,6 +91,19 @@
     def wait(ref, sem):
         pltpu.make_async_copy(ref, ref, sem).wait()
 
+    fetches = [
+        pltpu.make_async_copy(src, dst, in_sem.at[n])
+        for n, (src, dst) in enumerate(
+            (
+                (rec_hbm, rec_ref), (shapes_hbm, shapes_ref), (elem_hbm, elem_ref),
+                (coef_hbm, coef_ref), (first_hbm, first_ref), (bins_hbm, bins_ref),
+                (owner_hbm, owner_ref), (second_hbm, second_ref), (turn_hbm, turn_ref),
+            )
+        )
+    ]
+    for fetch in fetches:
+        fetch.start()
+
     barrier = pltpu.get_barrier_semaphore()
 
     def greet_plane(o, _):
@@ -111,12 +126,43 @@
         return pltpu.roll(tile, HALF, 1)
 
     pad_rec[...] = jnp.zeros_like(pad_rec)
+    fetches[0].wait()
     pad_rec[0:HALF, 0:MODES] = rec_ref[...].astype(f32)
     turned = pad_rec[...].T
     gathered[0] = (turned[0:FOLD] + swap(turned[FOLD : 2 * FOLD])).astype(bf16)
 
     shapes_out[MODES - 12 : 304, :] = jnp.zeros((16, E_DEV), bf16)
+    for fetch in fetches[1:4]:
+        fetch.wait()
     shapes_out[0:MODES, :] = shapes_ref[...]
+    pl.semaphore_wait(barrier, 38)
+
+    copies = []
+
+    def g_send(n, q, dq, j, device):
+        copies.append(
+            send(gathered.at[q * 4], gathered.at[dq * 4 + j], g_ss.at[n], g_rs.at[dq * 4 + j], device)
+        )
+
+    def g_wait(q, j):
+        wait(gathered.at[q * 4 + j], g_rs.at[q * 4 + j])
+
+    def v_send(q):
+        for j in (1, 3, 2):
+            g_send(3 * q + j - 1, q, q, j, line(core, u, lax.rem(v + 4 - j, 4), z, core))
+
+    def z_send(n, q, dq, dz, rows=None):
+        src, dst = gathered.at[q * 4], gathered.at[dq * 4]
+        rs = g_rs.at[dq * 4]
+        if rows is not None:
+            src, dst = src.at[pl.ds(rows, FOLD // 2)], dst.at[pl.ds(rows, FOLD // 2)]
+            rs = far_rs.at[rows // (FOLD // 2)]
+        copies.append(send(src, dst, z_ss.at[n], rs, at(x, y, lax.rem(z + 8 + dz, 8), core)))
+
+    for n, dz in enumerate((1, 7, 2, 6)):
+        z_send(n, 0, PLANE_AT[dz], -dz)
+    v_send(0)
+
     slots = pl.ds(pl.multiple_of(z_half * 128, 128), 128)
     elems = elem_ref[:, slots]
     coefs = coef_ref[:, slots]
@@ -135,6 +181,48 @@
 
     lax.fori_loop(0, 64, spread, 0)
 
+    def c_send(o, _):
+        to = lax.rem(ha + o, 32)
+        pltpu.make_async_remote_copy(
+            src_ref=c_out.at[pl.ds(2 * to, 2)], dst_ref=c_in.at[pl.ds(2 * (32 - o), 2)],
+            send_sem=c_ss, recv_sem=c_rs, device_id=(z, to), device_id_type=MESH,
+        ).start()
+        return 0
+
+    lax.fori_loop(1, 32, c_send, 0)
+    c_in[0] = c_out[2 * ha]
+    c_in[1] = c_out[2 * ha + 1]
+
+    owns = core == z_odd
+    shp_to = [
+        line(0, lax.rem(x + 4 - z_half, 4), y, z, 0),
+        line(1, lax.rem(y + 4 - z_half, 4), x, z, 1),
+    ]
+
+    def shape_copies(act):
+        for cc in range(2):
+            own_work = jnp.logical_and(z_half == 0, core == cc)
+
+            @pl.when(jnp.logical_and(owns, jnp.logical_not(own_work)))
+            def _():
+                act(
+                    pltpu.make_async_remote_copy(
+                        src_ref=shapes_out, dst_ref=shapes_in, send_sem=shp_ss.at[cc],
+                        recv_sem=shp_rs, device_id=shp_to[cc], device_id_type=MESH,
+                    )
+                )
+
+    shape_copies(lambda copy: copy.start())
+    local_shapes = jnp.logical_and(owns, z_half == 0)
+
+    @pl.when(local_shapes)
+    def _():
+        shapes_in[...] = shapes_out[...]
+
+    for q in (PLANE_AT[1], PLANE_AT[7]):
+        g_wait(q, 0)
+        v_send(q)
+
     col = lax.broadcasted_iota(i32, (128, 128), 1)
     row = lax.broadcasted_iota(i32, (128, 128), 0)
     source, place, dv = lax.div(col, 32), lax.div(lax.rem(col, 32), 4), lax.rem(col, 4)
@@ -144,86 +232,13 @@
     zz = lax.rem(z + dz, 8)
     a_even = 16 * zz + 4 * lax.rem(x + source, 4) + lax.rem(y + dv, 4)
     a_odd = 16 * zz + 4 * lax.rem(x + dv, 4) + lax.rem(y + source, 4)
+    fetches[4].wait()
     for half, a_of in enumerate((a_even, a_odd)):
         order = (row == a_of).astype(f32).astype(bf16)
         table[half] = jnp.dot(first_ref[...], order, preferred_element_type=f32).astype(bf16)
 
-    pl.semaphore_wait(barrier, 38)
-
-    copies = []
-    g_count = [0]
-
-    def g_send(q, j, rows, dq, dj, device):
-        n = g_count[0]
-        g_count[0] += 1
-        copies.append(
-            send(
-                gathered.at[q * 4 + j], gathered.at[dq * 4 + dj], g_ss.at[n],
-                g_rs.at[dq * 4 + dj], device,
-            )
-        )
-
-    up, down = lax.rem(z + 1, 8), lax.rem(z + 7, 8)
-
-    def z_send(k, j, go_up):
-        here = (8 - k) % 8 if go_up else k
-        there = (8 - k - 1) % 8 if go_up else k + 1
-        g_send(
-            PLANE_AT[here], j, None, PLANE_AT[there], j,
-            line(core, u, v, up if go_up else down, core),
-        )
-
-    def g_wait(q, j):
-        wait(gathered.at[q * 4 + j], g_rs.at[q * 4 + j])
-
-    for j in (1, 3, 2):
-        g_send(0, 0, None, 0, j, line(core, u, lax.rem(v + 4 - j, 4), z, core))
-    z_send(0, 0, True)
-    z_send(0, 0, False)
-
-    def c_send(o, _):
-        to = lax.rem(ha + o, 32)
-        pltpu.make_async_remote_copy(
-            src_ref=c_out.at[pl.ds(2 * to, 2)], dst_ref=c_in.at[pl.ds(2 * (32 - o), 2)],
-            send_sem=c_ss, recv_sem=c_rs, device_id=(z, to), device_id_type=MESH,
-        ).start()
-        return 0
-
-    lax.fori_loop(1, 32, c_send, 0)
-    c_in[0] = c_out[2 * ha]
-    c_in[1] = c_out[2 * ha + 1]
-
-    owns = core == z_odd
-    shp_to = [
-        line(0, lax.rem(x + 4 - z_half, 4), y, z, 0),
-        line(1, lax.rem(y + 4 - z_half, 4), x, z, 1),
-    ]
-
-    def shape_copies(act):
-        for cc in range(2):
-            own_work = jnp.logical_and(z_half == 0, core == cc)
-
-            @pl.when(jnp.logical_and(owns, jnp.logical_not(own_work)))
-            def _():
-                act(
-                    pltpu.make_async_remote_copy(
-                        src_ref=shapes_out, dst_ref=shapes_in, send_sem=shp_ss.at[cc],
-                        recv_sem=shp_rs, device_id=shp_to[cc], device_id_type=MESH,
-                    )
-                )
-
-    shape_copies(lambda copy: copy.start())
-    local_shapes = jnp.logical_and(owns, z_half == 0)
-
-    @pl.when(local_shapes)
-    def _():
-        shapes_in[...] = shapes_out[...]
-
-    for j in (1, 3, 2):
-        g_wait(0, j)
-        z_send(0, j, True)
-        z_send(0, j, False)
-
+    for fetch in fetches[5:]:
+        fetch.wait()
     bins = bins_ref[...].astype(f32)
     before = (
         lax.broadcasted_iota(i32, (NB, NB), 0) < lax.broadcasted_iota(i32, (NB, NB), 1)
@@ -241,17 +256,12 @@
         member[pl.ds(pl.multiple_of(i * 256, 256), 256), :] = inside.astype(f32).astype(bf16)
         return 0
 
-    lax.fori_loop(0, 16, member_block, 0)
-
-    def step(k):
-        for j in (0, 1, 3, 2):
-            for go_up in (True, False):
-                here = (8 - k) % 8 if go_up else k
-                g_wait(PLANE_AT[here], j)
-                if k < 3 or (j in (0, 1)) == go_up:
-                    z_send(k, j, go_up)
-
-    step(1)
+    for n, (dz, step) in enumerate(((2, -1), (6, 1))):
+        q = PLANE_AT[dz]
+        g_wait(q, 0)
+        z_send(4 + 2 * n, q, PLANE_AT[(dz - step) % 8], step)
+        z_send(5 + 2 * n, q, PLANE_AT[4], 2 * step, n * (FOLD // 2))
+        v_send(q)
 
     wait(c_in.at[pl.ds(2, 62)], c_rs)
 
@@ -294,8 +304,14 @@
         send(hot_mine, hot_in.at[core], hot_ss.at[0], hot_rs.at[core], at(x, y, z, 1 - core))
     )
 
-    lax.fori_loop(16, 32, member_block, 0)
-    step(2)
+    for q in (PLANE_AT[3], PLANE_AT[5]):
+        g_wait(q, 0)
+        v_send(q)
+    for n in range(2):
+        wait(gathered.at[PLANE_AT[4] * 4, pl.ds(n * (FOLD // 2), FOLD // 2)], far_rs.at[n])
+    v_send(PLANE_AT[4])
+
+    lax.fori_loop(0, 32, member_block, 0)
 
     @pl.when(jnp.logical_not(local_shapes))
     def _():
@@ -319,20 +335,20 @@
             )
         first = jnp.concatenate([parts[0][0], parts[1][0]], axis=1)
         last = jnp.concatenate([parts[0][1], parts[1][1]], axis=1)
-        wide[0:160, :] = first
-        wide[160:320, :] = last
-        wide[320:384, :] = last[96:160]
-        wide[384:544, :] = first
-        wide[544:640, :] = last[0:96]
-
-    def energies():
-        stress = jnp.dot(shapes_t[...], wide[0:384, :], preferred_element_type=f32)
+        wide[q, 0:160, :] = first
+        wide[q, 160:320, :] = last
+        wide[q, 320:384, :] = last[96:160]
+        wide[q, 384:544, :] = first
+        wide[q, 544:640, :] = last[0:96]
+
+    def energies(q):
+        stress = jnp.dot(shapes_t[...], wide[q, 0:384, :], preferred_element_type=f32)
         squares = stress * stress
         e_acc[...] += squares[:, 0:128] + squares[:, 128:256]
 
     def series(q):
         out = jnp.dot(
-            hot_in[...].reshape(256, 640), wide[...], preferred_element_type=f32
+            hot_in[...].reshape(256, 640), wide[q], preferred_element_type=f32
         ).reshape(8, 2, 16, 256)
         for pair in range(2):
             lanes = slice(pair * 128, pair * 128 + 128)
@@ -371,22 +387,15 @@
             wait(hot_in.at[du * 2 + cc], hot_rs.at[du * 2 + cc])
     wait(hot_in.at[1 - core], hot_rs.at[1 - core])
 
-    for q in range(4):
-        unfold(q)
-        series(q)
-        energies()
-    s_send(0)
-    step(3)
-    for q in range(4, 7):
-        unfold(q)
-        series(q)
-        energies()
-    for j in range(4):
-        g_wait(7, j)
-    unfold(7)
-    series(7)
-    s_send(1)
-    energies()
+    for piece in range(2):
+        for q in range(4 * piece, 4 * piece + 4):
+            for j in (1, 3, 2):
+                g_wait(q, j)
+            unfold(q)
+            series(q)
+        s_send(piece)
+        for q in range(4 * piece, 4 * piece + 4):
+            energies(q)
 
     e_mine[0] = jnp.sum(e_acc[...].T, axis=0, keepdims=True)
     e_local = jnp.logical_and(z_half == 0, core == z_odd)
@@ -423,26 +432,29 @@
 
             lax.fori_loop(1, 8, one, 0)
 
-    @pl.when(owns)
-    def _():
-        for cc in range(2):
-
-            @pl.when(jnp.logical_not(jnp.logical_and(z_half == 0, core == cc)))
-            def _():
-                wait(e_in.at[pl.ds(cc, 1)], e1_rs.at[cc])
-
-        e_sum[0] = e_in[0] + e_in[1]
-        e_all[z_half] = e_sum[0]
-
-    e_second(lambda copy: copy.start())
-
-    for piece in range(2):
+    def a_wait(piece):
         for half in range(2):
             for du in range(1, 4):
                 wait(arrived.at[half, du, piece], s_rs.at[half, du, piece])
         wait(arrived.at[1 - core, 0, piece], s_rs.at[1 - core, 0, piece])
 
-    def spectrum(pp, _):
+    a_wait(0)
+
+    @pl.when(owns)
+    def _():
+        for cc in range(2):
+
+            @pl.when(jnp.logical_not(jnp.logical_and(z_half == 0, core == cc)))
+            def _():
+                wait(e_in.at[pl.ds(cc, 1)], e1_rs.at[cc])
+
+        e_sum[0] = e_in[0] + e_in[1]
+        e_all[z_half] = e_sum[0]
+
+    e_second(lambda copy: copy.start())
+
+    a_wait(1)
+    for pp in range(8):
         ones = []
         for half in range(2):
             tiles = []
@@ -457,26 +469,31 @@
                         axis=0,
                     )
                 )
-            one = jnp.dot(
-                table[half], jnp.concatenate(tiles, axis=1), preferred_element_type=f32
+            ones.append(
+                jnp.dot(table[half], jnp.concatenate(tiles, axis=1), preferred_element_type=f32)
             )
-            ones.append(one)
         for n in range(2):
             lanes = slice(n * 128, n * 128 + 128)
-            blocks = []
             for half in range(2):
                 real, imag = ones[half][0:128, lanes], ones[half][128:256, lanes]
                 c, s = turn_ref[2 * half], turn_ref[2 * half + 1]
-                blocks += [(real * c + imag * s).astype(bf16), (imag * c - real * s).astype(bf16)]
-            out = jnp.dot(
-                jnp.concatenate(blocks, axis=1), second_ref[...], preferred_element_type=f32
-            )
-            real, imag = out[:, 0:128], out[:, 128:256]
-            power[pl.ds(2 * pp + n, 128, stride=16), :] = real * real + imag * imag
-        return 0
-
-    lax.fori_loop(0, 8, spectrum, 0)
-
+                rows = slice((2 * pp + n) * 128, (2 * pp + n) * 128 + 128)
+                twiddled[rows, half * 256 : half * 256 + 128] = (real * c + imag * s).astype(bf16)
+                twiddled[rows, half * 256 + 128 : half * 256 + 256] = (
+                    imag * c - real * s
+                ).astype(bf16)
+
+    second = second_ref[...].astype(bf16)
+    for chunk in range(4):
+        out = jnp.dot(
+            twiddled[chunk * 512 : chunk * 512 + 512, :], second, preferred_element_type=f32
+        )
+        real, imag = out[:, 0:128], out[:, 128:256]
+        squares = real * real + imag * imag
+        for n in range(4):
+            power[pl.ds(4 * chunk + n, 128, stride=16), :] = squares[n * 128 : n * 128 + 128]
+
+    sums = jnp.zeros((HS_DEV, NB), f32)
     for kb in range(32):
         tiles = []
         for pair in range(2):
@@ -487,8 +504,12 @@
                     [jnp.where(left, even, swap(odd)), jnp.where(left, swap(even), odd)], axis=0
                 )
             )
-        power_rows[:, kb * 256 : kb * 256 + 256] = jnp.concatenate(tiles, axis=1).astype(bf16)
-    band_ref[...] = jnp.dot(power_rows[...], member[...], preferred_element_type=f32)
+        sums = sums + jnp.dot(
+            jnp.concatenate(tiles, axis=1).astype(bf16),
+            member[kb * 256 : kb * 256 + 256, :],
+            preferred_element_type=f32,
+        )
+    band_ref[...] = sums / (NT * bins)
 
     for i in range(4):
 
@@ -496,7 +517,7 @@
         def _():
             wait(e_all.at[pl.ds(i, 1)], e2_rs.at[i])
 
-    energy_ref[...] = (e_all[0] + e_all[1]) + (e_all[2] + e_all[3])
+    energy_ref[...] = jnp.sqrt(((e_all[0] + e_all[1]) + (e_all[2] + e_all[3])) / NT + epsilon).reshape(E_DEV)
 
     for copy in copies:
         copy.wait_send()
@@ -511,6 +532,15 @@
     first, turn, second = tables()
     vmem, dma = pltpu.VMEM, pltpu.SemaphoreType.DMA
     scratch = [
+        vmem((HALF, MODES), bf16),
+        vmem((MODES, E_DEV), bf16),
+        vmem(map_elem.shape, jnp.int32),
+        vmem(map_coef.shape, f32),
+        vmem((1, HS_DEV), jnp.int32),
+        vmem((1, NB), jnp.int32),
+        vmem(first.shape, bf16),
+        vmem(turn.shape, f32),
+        vmem(second.shape, f32),
         vmem((128, 384), f32),
         vmem((384, 384), f32),
         vmem((304, 384), bf16),
@@ -523,43 +553,42 @@
         vmem((32, 640), bf16),
         vmem((8, 32, 640), bf16),
         vmem((32, FOLD, 128), bf16),
-        vmem((640, 256), bf16),
+        vmem((8, 640, 256), bf16),
         vmem((2048, 128), f32),
         vmem((2, 8, 16, 16, 128), bf16),
         vmem((2, 4, 2, 16, 16, 128), bf16),
         vmem((NT // 2, NB), bf16),
+        vmem((2048, 512), bf16),
         vmem((2048, 128), f32),
-        vmem((32, NT // 2), bf16),
         vmem((2, 256, 128), bf16),
         vmem((384, 128), f32),
         vmem((1, 1, 384), f32),
         vmem((2, 1, 384), f32),
         vmem((1, 1, 384), f32),
         vmem((4, 1, 384), f32),
-        dma((2,)), dma, dma, dma, dma((8,)), dma((8,)), dma((31,)), dma((32,)),
+        dma((2,)), dma, dma, dma, dma((8,)), dma((8,)), dma((24,)), dma((32,)), dma((8,)), dma((2,)),
         dma((2, 8)), dma((2, 4, 2)), dma, dma((2,)), dma((8,)), dma((4,)),
+        dma((9,)),
     ]
     whole = pl.BlockSpec(memory_space=pltpu.VMEM)
     sums, energy = pl.pallas_call(
         kernel,
         out_shape=(
-            jax.ShapeDtypeStruct((HS_DEV, NB), f32),
-            jax.ShapeDtypeStruct((1, E_DEV), f32),
+            pltpu.VMEM((HS_DEV, NB), f32),
+            pltpu.VMEM((E_DEV,), f32),
         ),
-        in_specs=[whole] * 9,
+        in_specs=[pl.BlockSpec(memory_space=pltpu.HBM)] * 9,
         out_specs=(whole, whole),
         scratch_shapes=scratch,
         compiler_params=pltpu.CompilerParams(
-            collective_id=0, has_side_effects=True, vmem_limit_bytes=48 * 2**20
+            collective_id=0, has_side_effects=True, vmem_limit_bytes=255 * 2**18
         ),
         name="whipping",
     )(
         mode_record.T, mode_shapes, map_elem, map_coef, hot_owner.reshape(1, HS_DEV),
         band_bins.reshape(1, NB), jnp.asarray(first), jnp.asarray(turn), jnp.asarray(second),
     )
-    elem_rms = jnp.sqrt(energy.reshape(E_DEV) / NT + epsilon)
-    band_power = sums / (NT * band_bins.astype(f32))[None, :]
-    return (elem_rms, band_power)
+    return (energy, sums)
 
 
 def solution(mesh):

time: 51.7 us -> 42.5 us (0.82)
  local copies, waits for them, and re-layouts: 6.54 us -> 1.21 us
  Pallas kernels: 42.9 us -> 40.5 us
  other arithmetic: 1.25 us -> 0 us
    unnamed x18 -> x2, local copies, waits for them, and re-layouts: 6.54 us -> 1.21 us
    pallas_call x1, Pallas kernels: 42.9 us -> 40.5 us  [shards(): pl.pallas_call(kernel, out_shape=(pltpu.VMEM((HS_DEV, NB), f32), pltpu.VM...]
    div x1 -> x0, other arithmetic: 0.64 us -> none  [shards(): band_power = sums / (NT * band_bins.astype(f32))[None, :]]
    sqrt x1 -> x0, other arithmetic: 0.6 us -> none  [shards(): elem_rms = jnp.sqrt(energy.reshape(E_DEV) / NT + epsilon)]
where the time goes in v2:
time: 42.5 us; the launch traced here: 42.4 us
  Pallas kernels  40.5 us (95%)
  local copies, waits for them, and re-layouts  1.21 us (3%)
  between operations  0.64 us (2%)
    pallas_call x1, Pallas kernels, shards(): pl.pallas_call(kernel, out_shape=(pltpu.VMEM((HS_DEV, NB), f32), pltpu.VM...  40.5 us
    unnamed x2, local copies, waits for them, and re-layouts  1.21 us

profile of v2, /device:TPU:1, one launch (start us, length us, event | category | flops | bytes accessed | tf_op | source)
XLA Modules:
  0.0 42.4 jit_solution(16038543956365317546)
XLA Ops:
  0.6 40.5 %whipping.1 = (f32[32,512]{1,0:T(8,128)S(1)}, f32[384]{0:T(512)S(1)}) custom-call(bf16[64,300]{1,0:T(8,128)(2,1)} %bitcast.3, bf16[300,384]{1,0:T(8,128)(2,1)} %shapes_hbm.1, s32[4,512]{1,0:T(4,128)} %elem_hbm.1, f32[4,512]{1,0:T(4,128)} %coef_hbm.1, s32[1,32]{1,0:T(1,128)} %bitcast.5, s32[1,512]{1,0:T(1,128)} %bitcast.4, ...), custom_call_target="tpu_custom_call" | custom-call | tf_op jit(solution)/shard_map/whipping/pallas_call | solution.py:574
  41.2 0.6 %copy.13 = f32[384]{0:T(512)} copy(f32[384]{0:T(512)S(1)} %get-tuple-element.6) | data formatting | bytes 3072
  41.7 0.6 %copy.14 = f32[32,512]{1,0:T(8,128)} copy(f32[32,512]{1,0:T(8,128)S(1)} %get-tuple-element.7) | data formatting | bytes 131072

commit v3 on v2

--- a/solution.py
+++ b/solution.py
@@ -14,6 +14,7 @@
 MODES = 300
 E_DEV = 384
 FOLD = 160
+SPLIT = 96
 KPAD = 320
 HALF = 64
 
@@ -57,10 +58,10 @@
     band_ref, energy_ref,
     rec_ref, shapes_ref, elem_ref, coef_ref, owner_ref, bins_ref, first_ref, turn_ref, second_ref,
     pad_rec, pad_shapes, shapes_out, shapes_in, shapes_t,
-    c_rows, c_out, c_in, c_flat, hot_mine, hot_in,
+    c_rows, c_out, c_mid, c_next, c_flat, hot_mine, hot_in,
     gathered, wide, folded, sending, arrived,
     member, twiddled, power, table, e_acc, e_mine, e_in, e_sum, e_all,
-    shp_ss, shp_rs, c_ss, c_rs, hot_ss, hot_rs, g_ss, g_rs, z_ss, far_rs, s_ss, s_rs, e1_ss, e1_rs, e2_ss, e2_rs,
+    shp_ss, shp_rs, c1_ss, c1_rs, c2_ss, c2_rs, hot_ss, hot_rs, g_ss, g_rs, z_ss, far_rs, h_ss, h_rs, s_ss, s_rs, e1_ss, e1_rs, e2_ss, e2_rs,
     in_sem,
 ):
     f32, bf16, i32 = jnp.float32, jnp.bfloat16, jnp.int32
@@ -106,18 +107,14 @@
 
     barrier = pltpu.get_barrier_semaphore()
 
-    def greet_plane(o, _):
-        pl.semaphore_signal(
-            barrier, inc=1, device_id=(z, lax.rem(ha + o, 32)), device_id_type=MESH
-        )
-        return 0
-
-    def greet_line(o, _):
-        pl.semaphore_signal(barrier, inc=1, device_id=(lax.rem(z + o, 8), ha), device_id_type=MESH)
-        return 0
-
-    lax.fori_loop(1, 32, greet_plane, 0)
-    lax.fori_loop(1, 8, greet_line, 0)
+    partners = [at(x, y, lax.rem(z + dz, 8), core) for dz in (1, 7, 2, 6)]
+    for d in (1, 3, 2):
+        for pc in range(2):
+            partners.append(at(x, lax.rem(y + d, 4), z, pc))
+            partners.append(at(lax.rem(x + d, 4), y, z, pc))
+    partners.append(at(x, y, z, 1 - core))
+    for partner in partners:
+        pl.semaphore_signal(barrier, inc=1, device_id=partner, device_id_type=MESH)
 
     lane128 = lax.broadcasted_iota(i32, (1, 128), 1)
     left = lane128 < HALF
@@ -135,34 +132,6 @@
     for fetch in fetches[1:4]:
         fetch.wait()
     shapes_out[0:MODES, :] = shapes_ref[...]
-    pl.semaphore_wait(barrier, 38)
-
-    copies = []
-
-    def g_send(n, q, dq, j, device):
-        copies.append(
-            send(gathered.at[q * 4], gathered.at[dq * 4 + j], g_ss.at[n], g_rs.at[dq * 4 + j], device)
-        )
-
-    def g_wait(q, j):
-        wait(gathered.at[q * 4 + j], g_rs.at[q * 4 + j])
-
-    def v_send(q):
-        for j in (1, 3, 2):
-            g_send(3 * q + j - 1, q, q, j, line(core, u, lax.rem(v + 4 - j, 4), z, core))
-
-    def z_send(n, q, dq, dz, rows=None):
-        src, dst = gathered.at[q * 4], gathered.at[dq * 4]
-        rs = g_rs.at[dq * 4]
-        if rows is not None:
-            src, dst = src.at[pl.ds(rows, FOLD // 2)], dst.at[pl.ds(rows, FOLD // 2)]
-            rs = far_rs.at[rows // (FOLD // 2)]
-        copies.append(send(src, dst, z_ss.at[n], rs, at(x, y, lax.rem(z + 8 + dz, 8), core)))
-
-    for n, dz in enumerate((1, 7, 2, 6)):
-        z_send(n, 0, PLANE_AT[dz], -dz)
-    v_send(0)
-
     slots = pl.ds(pl.multiple_of(z_half * 128, 128), 128)
     elems = elem_ref[:, slots]
     coefs = coef_ref[:, slots]
@@ -173,55 +142,16 @@
         hot = hot + coefs[k : k + 1, :] * jnp.dot(
             shapes_out[...], pick, preferred_element_type=f32
         )
-    c_rows[...] = jnp.concatenate([hot, jnp.zeros((80, 128), f32)], axis=0).T
-
-    def spread(i, _):
-        c_out[i] = c_rows[pl.ds(z_odd * HALF + i, 1), :]
-        return 0
-
-    lax.fori_loop(0, 64, spread, 0)
-
-    def c_send(o, _):
-        to = lax.rem(ha + o, 32)
-        pltpu.make_async_remote_copy(
-            src_ref=c_out.at[pl.ds(2 * to, 2)], dst_ref=c_in.at[pl.ds(2 * (32 - o), 2)],
-            send_sem=c_ss, recv_sem=c_rs, device_id=(z, to), device_id_type=MESH,
-        ).start()
-        return 0
-
-    lax.fori_loop(1, 32, c_send, 0)
-    c_in[0] = c_out[2 * ha]
-    c_in[1] = c_out[2 * ha + 1]
-
-    owns = core == z_odd
-    shp_to = [
-        line(0, lax.rem(x + 4 - z_half, 4), y, z, 0),
-        line(1, lax.rem(y + 4 - z_half, 4), x, z, 1),
-    ]
-
-    def shape_copies(act):
-        for cc in range(2):
-            own_work = jnp.logical_and(z_half == 0, core == cc)
-
-            @pl.when(jnp.logical_and(owns, jnp.logical_not(own_work)))
-            def _():
-                act(
-                    pltpu.make_async_remote_copy(
-                        src_ref=shapes_out, dst_ref=shapes_in, send_sem=shp_ss.at[cc],
-                        recv_sem=shp_rs, device_id=shp_to[cc], device_id_type=MESH,
-                    )
-                )
-
-    shape_copies(lambda copy: copy.start())
-    local_shapes = jnp.logical_and(owns, z_half == 0)
-
-    @pl.when(local_shapes)
-    def _():
-        shapes_in[...] = shapes_out[...]
-
-    for q in (PLANE_AT[1], PLANE_AT[7]):
-        g_wait(q, 0)
-        v_send(q)
+    hot = jnp.concatenate([hot, jnp.zeros((80, 128), f32)], axis=0).T
+    for t in range(3):
+        c_rows[t * 128 : t * 128 + 128, :] = hot[:, t * 128 : t * 128 + 128]
+
+    for g in range(8):
+        for t in range(3):
+            for rank in range(2):
+                start = t * 128 + z_odd * HALF + 16 * (g // 2) + 2 * (g % 2) + rank
+                to = (g * 3 + t) * 8 + rank * 4
+                c_out[to : to + 4, :] = c_rows[pl.ds(start, 4, stride=4), :]
 
     col = lax.broadcasted_iota(i32, (128, 128), 1)
     row = lax.broadcasted_iota(i32, (128, 128), 0)
@@ -256,20 +186,150 @@
         member[pl.ds(pl.multiple_of(i * 256, 256), 256), :] = inside.astype(f32).astype(bf16)
         return 0
 
+    pl.semaphore_wait(barrier, len(partners))
+
+    copies = []
+
+    first_rows, last_rows = pl.ds(0, SPLIT), pl.ds(SPLIT, FOLD - SPLIT)
+
+    def a_wait_first(q, j):
+        wait(gathered.at[q * 4 + j, first_rows], g_rs.at[q * 4 + j])
+
+    def a_wait_last(q, j):
+        wait(gathered.at[q * 4 + j, last_rows], h_rs.at[q * 4 + j])
+
+    def v_send(q):
+        for j in (1, 3, 2):
+            copies.append(
+                send(
+                    gathered.at[q * 4, first_rows], gathered.at[q * 4 + j, first_rows],
+                    g_ss.at[3 * q + j - 1], g_rs.at[q * 4 + j],
+                    line(core, u, lax.rem(v + 4 - j, 4), z, core),
+                )
+            )
+
+    def z_send(n, q, dq, dz, rows=None):
+        src, dst = gathered.at[q * 4, first_rows], gathered.at[dq * 4, first_rows]
+        rs = g_rs.at[dq * 4]
+        if rows is not None:
+            part = pl.ds(rows * (SPLIT // 2), SPLIT // 2)
+            src, dst, rs = gathered.at[q * 4, part], gathered.at[dq * 4, part], far_rs.at[rows]
+        copies.append(send(src, dst, z_ss.at[n], rs, at(x, y, lax.rem(z + 8 + dz, 8), core)))
+
+    def last_v_send():
+        for j in (1, 3, 2):
+            copies.append(
+                send(
+                    gathered.at[0, last_rows], gathered.at[j, last_rows], h_ss.at[j - 1],
+                    h_rs.at[j], line(core, u, lax.rem(v + 4 - j, 4), z, core),
+                )
+            )
+
+    last_count = [3]
+
+    def last_z_send(dz, to, j):
+        q, dq = PLANE_AT[dz % 8], PLANE_AT[(dz - to) % 8]
+        n = last_count[0]
+        last_count[0] += 1
+        copies.append(
+            send(
+                gathered.at[q * 4 + j, last_rows], gathered.at[dq * 4 + j, last_rows], h_ss.at[n],
+                h_rs.at[dq * 4 + j], at(x, y, lax.rem(z + 8 + to, 8), core),
+            )
+        )
+
+    def last_near(j):
+        for to in (1, -1, 2, -2):
+            last_z_send(0, to, j)
+
+    def last_far(j):
+        a_wait_last(PLANE_AT[2], j)
+        last_z_send(2, -1, j)
+        if j in (0, 1):
+            last_z_send(2, -2, j)
+        a_wait_last(PLANE_AT[6], j)
+        last_z_send(-2, 1, j)
+        if j in (2, 3):
+            last_z_send(-2, 2, j)
+
+    def group(px, pc):
+        return pl.ds(pl.multiple_of(24 * (px * 2 + pc), 8), 24)
+
+    for dx in (1, 3, 2, 0):
+        for dc in range(2):
+            to_x, to_c = lax.rem(x + dx, 4), jnp.where(dc == 0, core, 1 - core)
+            if dx or dc:
+                g = ((4 - dx) % 4) * 2 + dc
+                send(
+                    c_out.at[group(to_x, to_c)], c_mid.at[pl.ds(24 * g, 24)], c1_ss, c1_rs,
+                    at(to_x, y, z, to_c),
+                )
+    c_mid[0:24, :] = c_out[group(x, core), :]
+
+    for n, dz in enumerate((1, 7, 2, 6)):
+        z_send(n, 0, PLANE_AT[dz], -dz)
+    last_v_send()
+    last_near(0)
+    v_send(0)
+
+    def c_pass():
+        wait(c_mid.at[pl.ds(24, 168)], c1_rs)
+        for dy in (1, 3, 2, 0):
+            to_y = lax.rem(y + dy, 4)
+            for t in range(3):
+                for rank in range(2):
+                    to = dy * 48 + t * 16 + rank * 8
+                    c_next[to : to + 8, :] = c_mid[
+                        pl.ds(t * 8 + rank * 4 + to_y, 8, stride=24), :
+                    ]
+            if dy:
+                send(
+                    c_next.at[pl.ds(dy * 48, 48)], c_flat.at[pl.ds((4 - dy) * 48, 48)], c2_ss,
+                    c2_rs, at(x, to_y, z, core),
+                )
+        c_flat[0:48, :] = c_next[0:48, :]
+
+    owns = core == z_odd
+    shp_to = [
+        line(0, lax.rem(x + 4 - z_half, 4), y, z, 0),
+        line(1, lax.rem(y + 4 - z_half, 4), x, z, 1),
+    ]
+
+    def shape_copies(act):
+        for cc in range(2):
+            own_work = jnp.logical_and(z_half == 0, core == cc)
+
+            @pl.when(jnp.logical_and(owns, jnp.logical_not(own_work)))
+            def _():
+                act(
+                    pltpu.make_async_remote_copy(
+                        src_ref=shapes_out, dst_ref=shapes_in, send_sem=shp_ss.at[cc],
+                        recv_sem=shp_rs, device_id=shp_to[cc], device_id_type=MESH,
+                    )
+                )
+
+    shape_copies(lambda copy: copy.start())
+    local_shapes = jnp.logical_and(owns, z_half == 0)
+
+    @pl.when(local_shapes)
+    def _():
+        shapes_in[...] = shapes_out[...]
+
+    for j in (1, 3, 2):
+        a_wait_last(0, j)
+        last_near(j)
+    for q in (PLANE_AT[1], PLANE_AT[7]):
+        a_wait_first(q, 0)
+        v_send(q)
+    c_pass()
     for n, (dz, step) in enumerate(((2, -1), (6, 1))):
         q = PLANE_AT[dz]
-        g_wait(q, 0)
+        a_wait_first(q, 0)
         z_send(4 + 2 * n, q, PLANE_AT[(dz - step) % 8], step)
-        z_send(5 + 2 * n, q, PLANE_AT[4], 2 * step, n * (FOLD // 2))
+        z_send(5 + 2 * n, q, PLANE_AT[4], 2 * step, n)
         v_send(q)
-
-    wait(c_in.at[pl.ds(2, 62)], c_rs)
-
-    def flatten(i, _):
-        c_flat[pl.ds(i, 1), :] = c_in[i]
-        return 0
-
-    lax.fori_loop(0, 64, flatten, 0)
+    last_far(0)
+    wait(c_flat.at[pl.ds(48, 144)], c2_rs)
     owner_row = owner_ref[...]
     r32 = lax.broadcasted_iota(i32, (32, 32), 0)
     c32 = lax.broadcasted_iota(i32, (32, 32), 1)
@@ -279,10 +339,21 @@
         jnp.logical_and(owners == owner_col, c32 < r32).astype(i32), axis=1, keepdims=True
     )
     slot = lax.broadcasted_iota(i32, (32, 64), 1)
-    region = lax.rem(ha + lax.div(slot, 2), 32)
-    chosen = jnp.logical_and(region == owner_col, lax.rem(slot, 2) == rank)
+    region_x = lax.rem(x + lax.rem(lax.div(slot, 2), 4), 4)
+    region_y = lax.rem(y + lax.div(slot, 16), 4)
+    region_c = lax.rem(core + lax.rem(slot, 2), 2)
+    region = (region_x * 4 + region_y) * 2 + region_c
+    chosen = jnp.logical_and(region == owner_col, lax.rem(lax.div(slot, 8), 2) == rank)
     chosen = chosen.astype(f32).astype(bf16)
-    flat = c_flat[...]
+    flat = jnp.concatenate(
+        [
+            jnp.concatenate(
+                [c_flat[e * 48 + t * 16 : e * 48 + t * 16 + 16, :] for e in range(4)], axis=0
+            )
+            for t in range(3)
+        ],
+        axis=1,
+    )
     high = flat.astype(bf16)
     low = (flat - high.astype(f32)).astype(bf16)
     high = jnp.dot(chosen, high, preferred_element_type=f32)
@@ -304,15 +375,16 @@
         send(hot_mine, hot_in.at[core], hot_ss.at[0], hot_rs.at[core], at(x, y, z, 1 - core))
     )
 
+
     for q in (PLANE_AT[3], PLANE_AT[5]):
-        g_wait(q, 0)
+        a_wait_first(q, 0)
         v_send(q)
     for n in range(2):
-        wait(gathered.at[PLANE_AT[4] * 4, pl.ds(n * (FOLD // 2), FOLD // 2)], far_rs.at[n])
+        part = pl.ds(n * (SPLIT // 2), SPLIT // 2)
+        wait(gathered.at[PLANE_AT[4] * 4, part], far_rs.at[n])
     v_send(PLANE_AT[4])
-
-    lax.fori_loop(0, 32, member_block, 0)
-
+    for j in (1, 3, 2):
+        last_far(j)
     @pl.when(jnp.logical_not(local_shapes))
     def _():
         wait(shapes_in, shp_rs)
@@ -382,20 +454,26 @@
             )
         )
 
+    def planes(piece):
+        for q in range(4 * piece, 4 * piece + 4):
+            for j in range(4):
+                if j:
+                    a_wait_first(q, j)
+                if q not in (PLANE_AT[0], PLANE_AT[2], PLANE_AT[6]):
+                    a_wait_last(q, j)
+            unfold(q)
+            energies(q)
+
+    planes(0)
     for du in range(1, 4):
         for cc in range(2):
             wait(hot_in.at[du * 2 + cc], hot_rs.at[du * 2 + cc])
     wait(hot_in.at[1 - core], hot_rs.at[1 - core])
 
-    for piece in range(2):
-        for q in range(4 * piece, 4 * piece + 4):
-            for j in (1, 3, 2):
-                g_wait(q, j)
-            unfold(q)
-            series(q)
-        s_send(piece)
-        for q in range(4 * piece, 4 * piece + 4):
-            energies(q)
+    for q in range(4):
+        series(q)
+    s_send(0)
+    planes(1)
 
     e_mine[0] = jnp.sum(e_acc[...].T, axis=0, keepdims=True)
     e_local = jnp.logical_and(z_half == 0, core == z_odd)
@@ -417,28 +495,46 @@
     def _():
         e_in[core] = e_mine[0]
 
-    def e_second(act):
-        @pl.when(owns)
-        def _():
-            def one(o, _):
-                act(
-                    pltpu.make_async_remote_copy(
-                        src_ref=e_sum, dst_ref=e_all.at[pl.ds(z_half, 1)], send_sem=e2_ss.at[o],
-                        recv_sem=e2_rs.at[z_half], device_id=(lax.rem(z + o, 8), ha),
-                        device_id_type=MESH,
-                    )
-                )
-                return 0
-
-            lax.fori_loop(1, 8, one, 0)
-
     def a_wait(piece):
         for half in range(2):
             for du in range(1, 4):
                 wait(arrived.at[half, du, piece], s_rs.at[half, du, piece])
         wait(arrived.at[1 - core, 0, piece], s_rs.at[1 - core, 0, piece])
 
-    a_wait(0)
+    for q in range(4, 8):
+        series(q)
+    s_send(1)
+
+    def e_slot(d):
+        return lax.div(lax.rem(z + d, 8), 2)
+
+    def e_wait(d):
+        wait(e_all.at[pl.ds(e_slot(d), 1)], e2_rs.at[e_slot(d)])
+
+    def e_copy(src, d, to, n):
+        return pltpu.make_async_remote_copy(
+            src_ref=src, dst_ref=e_all.at[pl.ds(e_slot(d), 1)], send_sem=e2_ss.at[n],
+            recv_sem=e2_rs.at[e_slot(d)], device_id=at(x, y, lax.rem(z + to, 8), core),
+            device_id_type=MESH,
+        )
+
+    def e_second(act):
+        @pl.when(owns)
+        def _():
+            for n, to in enumerate((1, 7, 2, 6)):
+                act(e_copy(e_sum, 0, to, n))
+
+    def e_third(act):
+        @pl.when(owns)
+        def _():
+            act(e_copy(e_all.at[pl.ds(e_slot(2), 1)], 2, 6, 4))
+
+        @pl.when(jnp.logical_not(owns))
+        def _():
+            act(e_copy(e_all.at[pl.ds(e_slot(1), 1)], 1, 6, 4))
+            act(e_copy(e_all.at[pl.ds(e_slot(7), 1)], 7, 2, 5))
+
+    lax.fori_loop(0, 16, member_block, 0)
 
     @pl.when(owns)
     def _():
@@ -452,6 +548,18 @@
         e_all[z_half] = e_sum[0]
 
     e_second(lambda copy: copy.start())
+    lax.fori_loop(16, 32, member_block, 0)
+    a_wait(0)
+    @pl.when(owns)
+    def _():
+        e_wait(2)
+
+    @pl.when(jnp.logical_not(owns))
+    def _():
+        e_wait(1)
+        e_wait(7)
+
+    e_third(lambda copy: copy.start())
 
     a_wait(1)
     for pp in range(8):
@@ -511,20 +619,26 @@
         )
     band_ref[...] = sums / (NT * bins)
 
-    for i in range(4):
-
-        @pl.when(jnp.logical_not(jnp.logical_and(owns, z_half == i)))
-        def _():
-            wait(e_all.at[pl.ds(i, 1)], e2_rs.at[i])
+    @pl.when(owns)
+    def _():
+        e_wait(6)
+        e_wait(4)
+
+    @pl.when(jnp.logical_not(owns))
+    def _():
+        e_wait(3)
+        e_wait(5)
 
     energy_ref[...] = jnp.sqrt(((e_all[0] + e_all[1]) + (e_all[2] + e_all[3])) / NT + epsilon).reshape(E_DEV)
 
     for copy in copies:
         copy.wait_send()
-    wait(c_out.at[pl.ds(2, 62)], c_ss)
+    wait(c_out.at[pl.ds(24, 168)], c1_ss)
+    wait(c_next.at[pl.ds(48, 144)], c2_ss)
     shape_copies(lambda copy: copy.wait_send())
     e_first(lambda copy: copy.wait_send())
     e_second(lambda copy: copy.wait_send())
+    e_third(lambda copy: copy.wait_send())
 
 
 def shards(mode_record, mode_shapes, map_elem, map_coef, hot_owner, band_bins):
@@ -546,10 +660,11 @@
         vmem((304, 384), bf16),
         vmem((304, 384), bf16),
         vmem((384, 384), bf16),
-        vmem((128, 384), f32),
-        vmem((64, 1, 384), f32),
-        vmem((64, 1, 384), f32),
-        vmem((64, 384), f32),
+        vmem((384, 128), f32),
+        vmem((192, 128), f32),
+        vmem((192, 128), f32),
+        vmem((192, 128), f32),
+        vmem((192, 128), f32),
         vmem((32, 640), bf16),
         vmem((8, 32, 640), bf16),
         vmem((32, FOLD, 128), bf16),
@@ -566,7 +681,7 @@
         vmem((2, 1, 384), f32),
         vmem((1, 1, 384), f32),
         vmem((4, 1, 384), f32),
-        dma((2,)), dma, dma, dma, dma((8,)), dma((8,)), dma((24,)), dma((32,)), dma((8,)), dma((2,)),
+        dma((2,)), dma, dma, dma, dma, dma, dma((8,)), dma((8,)), dma((24,)), dma((32,)), dma((8,)), dma((2,)), dma((31,)), dma((32,)),
         dma((2, 8)), dma((2, 4, 2)), dma, dma((2,)), dma((8,)), dma((4,)),
         dma((9,)),
     ]

time: 42.5 us -> 40.8 us (0.960)
  Pallas kernels: 40.5 us -> 38.9 us
    pallas_call x1, Pallas kernels: 40.5 us -> 38.9 us  [shards(): pl.pallas_call(kernel, out_shape=(pltpu.VMEM((HS_DEV, NB), f32), pltpu.VM...]
where the time goes in v3:
time: 40.8 us; the launch traced here: 40.7 us
  Pallas kernels  38.9 us (95%)
  local copies, waits for them, and re-layouts  1.21 us (3%)
  between operations  0.64 us (2%)
    pallas_call x1, Pallas kernels, shards(): pl.pallas_call(kernel, out_shape=(pltpu.VMEM((HS_DEV, NB), f32), pltpu.VM...  38.9 us
    unnamed x2, local copies, waits for them, and re-layouts  1.21 us

profile of v3, /device:TPU:1, one launch (start us, length us, event | category | flops | bytes accessed | tf_op | source)
XLA Modules:
  0.0 40.7 jit_solution(11998688976457158943)
XLA Ops:
  0.6 38.9 %whipping.1 = (f32[32,512]{1,0:T(8,128)S(1)}, f32[384]{0:T(512)S(1)}) custom-call(bf16[64,300]{1,0:T(8,128)(2,1)} %bitcast.3, bf16[300,384]{1,0:T(8,128)(2,1)} %shapes_hbm.1, s32[4,512]{1,0:T(4,128)} %elem_hbm.1, f32[4,512]{1,0:T(4,128)} %coef_hbm.1, s32[1,32]{1,0:T(1,128)} %bitcast.5, s32[1,512]{1,0:T(1,128)} %bitcast.4, ...), custom_call_target="tpu_custom_call" | custom-call | tf_op jit(solution)/shard_map/whipping/pallas_call | solution.py:689
  39.5 0.6 %copy.13 = f32[384]{0:T(512)} copy(f32[384]{0:T(512)S(1)} %get-tuple-element.6) | data formatting | bytes 3072
  40.1 0.6 %copy.14 = f32[32,512]{1,0:T(8,128)} copy(f32[32,512]{1,0:T(8,128)S(1)} %get-tuple-element.7) | data formatting | bytes 131072

commit v4 on v3

--- a/solution.py
+++ b/solution.py
@@ -199,7 +199,7 @@
         wait(gathered.at[q * 4 + j, last_rows], h_rs.at[q * 4 + j])
 
     def v_send(q):
-        for j in (1, 3, 2):
+        for j in (2, 1, 3):
             copies.append(
                 send(
                     gathered.at[q * 4, first_rows], gathered.at[q * 4 + j, first_rows],
@@ -217,7 +217,7 @@
         copies.append(send(src, dst, z_ss.at[n], rs, at(x, y, lax.rem(z + 8 + dz, 8), core)))
 
     def last_v_send():
-        for j in (1, 3, 2):
+        for j in (2, 1, 3):
             copies.append(
                 send(
                     gathered.at[0, last_rows], gathered.at[j, last_rows], h_ss.at[j - 1],
@@ -255,7 +255,7 @@
     def group(px, pc):
         return pl.ds(pl.multiple_of(24 * (px * 2 + pc), 8), 24)
 
-    for dx in (1, 3, 2, 0):
+    for dx in (2, 1, 3, 0):
         for dc in range(2):
             to_x, to_c = lax.rem(x + dx, 4), jnp.where(dc == 0, core, 1 - core)
             if dx or dc:
@@ -274,7 +274,7 @@
 
     def c_pass():
         wait(c_mid.at[pl.ds(24, 168)], c1_rs)
-        for dy in (1, 3, 2, 0):
+        for dy in (2, 1, 3, 0):
             to_y = lax.rem(y + dy, 4)
             for t in range(3):
                 for rank in range(2):
@@ -318,10 +318,10 @@
     for j in (1, 3, 2):
         a_wait_last(0, j)
         last_near(j)
+    c_pass()
     for q in (PLANE_AT[1], PLANE_AT[7]):
         a_wait_first(q, 0)
         v_send(q)
-    c_pass()
     for n, (dz, step) in enumerate(((2, -1), (6, 1))):
         q = PLANE_AT[dz]
         a_wait_first(q, 0)
@@ -362,7 +362,7 @@
         [high[:, 0:256], high[:, 256:384] + swap(low[:, 256:384]), low[:, 0:256]], axis=1
     ).astype(bf16)
     hot_in[core] = hot_mine[...]
-    for du in range(1, 4):
+    for du in (2, 1, 3):
         for cc in range(2):
             here_u, here_v = (x, y) if cc == 0 else (y, x)
             copies.append(
@@ -437,7 +437,7 @@
     def s_send(piece):
         sending[piece] = folded[...].astype(bf16).reshape(8, 16, 16, 128)
         arrived[core, 0, piece] = sending[piece, core]
-        for du in range(1, 4):
+        for du in (2, 1, 3):
             for cc in range(2):
                 n = du * 2 + cc
                 copies.append(
@@ -534,7 +534,7 @@
             act(e_copy(e_all.at[pl.ds(e_slot(1), 1)], 1, 6, 4))
             act(e_copy(e_all.at[pl.ds(e_slot(7), 1)], 7, 2, 5))
 
-    lax.fori_loop(0, 16, member_block, 0)
+    lax.fori_loop(0, 10, member_block, 0)
 
     @pl.when(owns)
     def _():
@@ -548,7 +548,7 @@
         e_all[z_half] = e_sum[0]
 
     e_second(lambda copy: copy.start())
-    lax.fori_loop(16, 32, member_block, 0)
+    lax.fori_loop(10, 32, member_block, 0)
     a_wait(0)
     @pl.when(owns)
     def _():

time: 40.8 us -> 39.4 us (0.966)
  Pallas kernels: 38.9 us -> 37.5 us
    pallas_call x1, Pallas kernels: 38.9 us -> 37.5 us  [shards(): pl.pallas_call(kernel, out_shape=(pltpu.VMEM((HS_DEV, NB), f32), pltpu.VM...]
where the time goes in v4:
time: 39.4 us; the launch traced here: 39.3 us
  Pallas kernels  37.5 us (95%)
  local copies, waits for them, and re-layouts  1.21 us (3%)
  between operations  0.64 us (2%)
    pallas_call x1, Pallas kernels, shards(): pl.pallas_call(kernel, out_shape=(pltpu.VMEM((HS_DEV, NB), f32), pltpu.VM...  37.5 us
    unnamed x2, local copies, waits for them, and re-layouts  1.21 us

profile of v4, /device:TPU:1, one launch (start us, length us, event | category | flops | bytes accessed | tf_op | source)
XLA Modules:
  0.0 39.3 jit_solution(7468136311242016847)
XLA Ops:
  0.6 37.5 %whipping.1 = (f32[32,512]{1,0:T(8,128)S(1)}, f32[384]{0:T(512)S(1)}) custom-call(bf16[64,300]{1,0:T(8,128)(2,1)} %bitcast.3, bf16[300,384]{1,0:T(8,128)(2,1)} %shapes_hbm.1, s32[4,512]{1,0:T(4,128)} %elem_hbm.1, f32[4,512]{1,0:T(4,128)} %coef_hbm.1, s32[1,32]{1,0:T(1,128)} %bitcast.5, s32[1,512]{1,0:T(1,128)} %bitcast.4, ...), custom_call_target="tpu_custom_call" | custom-call | tf_op jit(solution)/shard_map/whipping/pallas_call | solution.py:689
  38.1 0.6 %copy.13 = f32[384]{0:T(512)} copy(f32[384]{0:T(512)S(1)} %get-tuple-element.6) | data formatting | bytes 3072
  38.7 0.6 %copy.14 = f32[32,512]{1,0:T(8,128)} copy(f32[32,512]{1,0:T(8,128)S(1)} %get-tuple-element.7) | data formatting | bytes 131072

commit v5 on v4

--- a/solution.py
+++ b/solution.py
@@ -186,6 +186,21 @@
         member[pl.ds(pl.multiple_of(i * 256, 256), 256), :] = inside.astype(f32).astype(bf16)
         return 0
 
+    owner_row = owner_ref[...]
+    r32 = lax.broadcasted_iota(i32, (32, 32), 0)
+    c32 = lax.broadcasted_iota(i32, (32, 32), 1)
+    owners = jnp.broadcast_to(owner_row, (32, 32))
+    owner_col = jnp.sum(jnp.where(r32 == c32, owners, 0), axis=1, keepdims=True)
+    rank = jnp.sum(
+        jnp.logical_and(owners == owner_col, c32 < r32).astype(i32), axis=1, keepdims=True
+    )
+    slot = lax.broadcasted_iota(i32, (32, 64), 1)
+    region_x = lax.rem(x + lax.rem(lax.div(slot, 2), 4), 4)
+    region_y = lax.rem(y + lax.div(slot, 16), 4)
+    region_c = lax.rem(core + lax.rem(slot, 2), 2)
+    region = (region_x * 4 + region_y) * 2 + region_c
+    chosen = jnp.logical_and(region == owner_col, lax.rem(lax.div(slot, 8), 2) == rank)
+    chosen = chosen.astype(f32).astype(bf16)
     pl.semaphore_wait(barrier, len(partners))
 
     copies = []
@@ -330,21 +345,6 @@
         v_send(q)
     last_far(0)
     wait(c_flat.at[pl.ds(48, 144)], c2_rs)
-    owner_row = owner_ref[...]
-    r32 = lax.broadcasted_iota(i32, (32, 32), 0)
-    c32 = lax.broadcasted_iota(i32, (32, 32), 1)
-    owners = jnp.broadcast_to(owner_row, (32, 32))
-    owner_col = jnp.sum(jnp.where(r32 == c32, owners, 0), axis=1, keepdims=True)
-    rank = jnp.sum(
-        jnp.logical_and(owners == owner_col, c32 < r32).astype(i32), axis=1, keepdims=True
-    )
-    slot = lax.broadcasted_iota(i32, (32, 64), 1)
-    region_x = lax.rem(x + lax.rem(lax.div(slot, 2), 4), 4)
-    region_y = lax.rem(y + lax.div(slot, 16), 4)
-    region_c = lax.rem(core + lax.rem(slot, 2), 2)
-    region = (region_x * 4 + region_y) * 2 + region_c
-    chosen = jnp.logical_and(region == owner_col, lax.rem(lax.div(slot, 8), 2) == rank)
-    chosen = chosen.astype(f32).astype(bf16)
     flat = jnp.concatenate(
         [
             jnp.concatenate(
@@ -356,12 +356,13 @@
     )
     high = flat.astype(bf16)
     low = (flat - high.astype(f32)).astype(bf16)
-    high = jnp.dot(chosen, high, preferred_element_type=f32)
-    low = jnp.dot(chosen, low, preferred_element_type=f32)
+    both = jnp.dot(
+        chosen, jnp.concatenate([high, low], axis=1), preferred_element_type=f32
+    )
+    high, low = both[:, 0:384], both[:, 384:768]
     hot_mine[...] = jnp.concatenate(
         [high[:, 0:256], high[:, 256:384] + swap(low[:, 256:384]), low[:, 0:256]], axis=1
     ).astype(bf16)
-    hot_in[core] = hot_mine[...]
     for du in (2, 1, 3):
         for cc in range(2):
             here_u, here_v = (x, y) if cc == 0 else (y, x)
@@ -374,6 +375,7 @@
     copies.append(
         send(hot_mine, hot_in.at[core], hot_ss.at[0], hot_rs.at[core], at(x, y, z, 1 - core))
     )
+    hot_in[core] = hot_mine[...]
 
 
     for q in (PLANE_AT[3], PLANE_AT[5]):

time: 39.4 us -> 39.1 us (level)
  no operation moved by 1% of the time
where the time goes in v5:
time: 39.1 us; the launch traced here: 39 us
  Pallas kernels  37.2 us (95%)
  local copies, waits for them, and re-layouts  1.21 us (3%)
  between operations  0.64 us (2%)
    pallas_call x1, Pallas kernels, shards(): pl.pallas_call(kernel, out_shape=(pltpu.VMEM((HS_DEV, NB), f32), pltpu.VM...  37.2 us
    unnamed x2, local copies, waits for them, and re-layouts  1.21 us

profile of v5, /device:TPU:1, one launch (start us, length us, event | category | flops | bytes accessed | tf_op | source)
XLA Modules:
  0.0 39.0 jit_solution(18193966918980238769)
XLA Ops:
  0.6 37.2 %whipping.1 = (f32[32,512]{1,0:T(8,128)S(1)}, f32[384]{0:T(512)S(1)}) custom-call(bf16[64,300]{1,0:T(8,128)(2,1)} %bitcast.3, bf16[300,384]{1,0:T(8,128)(2,1)} %shapes_hbm.1, s32[4,512]{1,0:T(4,128)} %elem_hbm.1, f32[4,512]{1,0:T(4,128)} %coef_hbm.1, s32[1,32]{1,0:T(1,128)} %bitcast.5, s32[1,512]{1,0:T(1,128)} %bitcast.4, ...), custom_call_target="tpu_custom_call" | custom-call | tf_op jit(solution)/shard_map/whipping/pallas_call | solution.py:691
  37.8 0.6 %copy.13 = f32[384]{0:T(512)} copy(f32[384]{0:T(512)S(1)} %get-tuple-element.6) | data formatting | bytes 3072
  38.4 0.6 %copy.14 = f32[32,512]{1,0:T(8,128)} copy(f32[32,512]{1,0:T(8,128)S(1)} %get-tuple-element.7) | data formatting | bytes 131072

commit v6 on v5

--- a/solution.py
+++ b/solution.py
@@ -153,39 +153,8 @@
                 to = (g * 3 + t) * 8 + rank * 4
                 c_out[to : to + 4, :] = c_rows[pl.ds(start, 4, stride=4), :]
 
-    col = lax.broadcasted_iota(i32, (128, 128), 1)
-    row = lax.broadcasted_iota(i32, (128, 128), 0)
-    source, place, dv = lax.div(col, 32), lax.div(lax.rem(col, 32), 4), lax.rem(col, 4)
-    dz = jnp.zeros_like(col)
-    for i, value in enumerate(PLANES):
-        dz = jnp.where(place == i, value, dz)
-    zz = lax.rem(z + dz, 8)
-    a_even = 16 * zz + 4 * lax.rem(x + source, 4) + lax.rem(y + dv, 4)
-    a_odd = 16 * zz + 4 * lax.rem(x + dv, 4) + lax.rem(y + source, 4)
-    fetches[4].wait()
-    for half, a_of in enumerate((a_even, a_odd)):
-        order = (row == a_of).astype(f32).astype(bf16)
-        table[half] = jnp.dot(first_ref[...], order, preferred_element_type=f32).astype(bf16)
-
     for fetch in fetches[5:]:
         fetch.wait()
-    bins = bins_ref[...].astype(f32)
-    before = (
-        lax.broadcasted_iota(i32, (NB, NB), 0) < lax.broadcasted_iota(i32, (NB, NB), 1)
-    ).astype(f32).astype(bf16)
-    starts = jnp.dot(
-        jnp.broadcast_to(bins, (8, NB)).astype(bf16), before, preferred_element_type=f32
-    )[0:1]
-    starts_i = starts.astype(i32)
-    ends_i = (starts + bins).astype(i32)
-
-    def member_block(i, _):
-        rows = lax.broadcasted_iota(i32, (256, 1), 0)
-        bin_ids = i * 4 + lax.div(rows, HALF) + DFT_LEN * lax.rem(rows, HALF)
-        inside = jnp.logical_and(bin_ids >= starts_i, bin_ids < ends_i)
-        member[pl.ds(pl.multiple_of(i * 256, 256), 256), :] = inside.astype(f32).astype(bf16)
-        return 0
-
     owner_row = owner_ref[...]
     r32 = lax.broadcasted_iota(i32, (32, 32), 0)
     c32 = lax.broadcasted_iota(i32, (32, 32), 1)
@@ -329,6 +298,37 @@
     @pl.when(local_shapes)
     def _():
         shapes_in[...] = shapes_out[...]
+
+    col = lax.broadcasted_iota(i32, (128, 128), 1)
+    row = lax.broadcasted_iota(i32, (128, 128), 0)
+    source, place, dv = lax.div(col, 32), lax.div(lax.rem(col, 32), 4), lax.rem(col, 4)
+    dz = jnp.zeros_like(col)
+    for i, value in enumerate(PLANES):
+        dz = jnp.where(place == i, value, dz)
+    zz = lax.rem(z + dz, 8)
+    a_even = 16 * zz + 4 * lax.rem(x + source, 4) + lax.rem(y + dv, 4)
+    a_odd = 16 * zz + 4 * lax.rem(x + dv, 4) + lax.rem(y + source, 4)
+    fetches[4].wait()
+    for half, a_of in enumerate((a_even, a_odd)):
+        order = (row == a_of).astype(f32).astype(bf16)
+        table[half] = jnp.dot(first_ref[...], order, preferred_element_type=f32).astype(bf16)
+
+    bins = bins_ref[...].astype(f32)
+    before = (
+        lax.broadcasted_iota(i32, (NB, NB), 0) < lax.broadcasted_iota(i32, (NB, NB), 1)
+    ).astype(f32).astype(bf16)
+    starts = jnp.dot(
+        jnp.broadcast_to(bins, (8, NB)).astype(bf16), before, preferred_element_type=f32
+    )[0:1]
+    starts_i = starts.astype(i32)
+    ends_i = (starts + bins).astype(i32)
+
+    def member_block(i, _):
+        rows = lax.broadcasted_iota(i32, (256, 1), 0)
+        bin_ids = i * 4 + lax.div(rows, HALF) + DFT_LEN * lax.rem(rows, HALF)
+        inside = jnp.logical_and(bin_ids >= starts_i, bin_ids < ends_i)
+        member[pl.ds(pl.multiple_of(i * 256, 256), 256), :] = inside.astype(f32).astype(bf16)
+        return 0
 
     for j in (1, 3, 2):
         a_wait_last(0, j)

time: 39.1 us -> 39.1 us (level)
  no operation moved by 1% of the time
where the time goes in v6:
time: 39.1 us; the launch traced here: 39 us
  Pallas kernels  37.2 us (95%)
  local copies, waits for them, and re-layouts  1.21 us (3%)
  between operations  0.64 us (2%)
    pallas_call x1, Pallas kernels, shards(): pl.pallas_call(kernel, out_shape=(pltpu.VMEM((HS_DEV, NB), f32), pltpu.VM...  37.2 us
    unnamed x2, local copies, waits for them, and re-layouts  1.21 us

profile of v6, /device:TPU:1, one launch (start us, length us, event | category | flops | bytes accessed | tf_op | source)
XLA Modules:
  0.0 39.0 jit_solution(2806052152087223985)
XLA Ops:
  0.6 37.2 %whipping.1 = (f32[32,512]{1,0:T(8,128)S(1)}, f32[384]{0:T(512)S(1)}) custom-call(bf16[64,300]{1,0:T(8,128)(2,1)} %bitcast.3, bf16[300,384]{1,0:T(8,128)(2,1)} %shapes_hbm.1, s32[4,512]{1,0:T(4,128)} %elem_hbm.1, f32[4,512]{1,0:T(4,128)} %coef_hbm.1, s32[1,32]{1,0:T(1,128)} %bitcast.5, s32[1,512]{1,0:T(1,128)} %bitcast.4, ...), custom_call_target="tpu_custom_call" | custom-call | tf_op jit(solution)/shard_map/whipping/pallas_call | solution.py:691
  37.8 0.6 %copy.13 = f32[384]{0:T(512)} copy(f32[384]{0:T(512)S(1)} %get-tuple-element.6) | data formatting | bytes 3072
  38.4 0.6 %copy.14 = f32[32,512]{1,0:T(8,128)} copy(f32[32,512]{1,0:T(8,128)S(1)} %get-tuple-element.7) | data formatting | bytes 131072
